TPU v7x, 32 devices: a whole 2x2x4 slice. The times are simulated.
32 devices in a mesh: wide: 16 (over z, y, core), narrow: 2 (over x).
Axes of the slice: x: 2, y: 2, z: 4, core: 2. Of those that a mesh axis runs over, the one named last changes fastest.
Arguments:
- adjoint_rhs: bfloat16 [16, 2, 768, 256], P('wide', 'narrow'), may hold values from -6 to 6
- inverse_rows: bfloat16 [16, 2, 768, 1024], P('wide', 'narrow'), may hold values from -0.2 to 1.2
- blocks: bfloat16 [16, 2, 6, 3, 128, 128], P('wide', 'narrow'), may hold values from -0.3 to 1.3
- block_cols: int32 [16, 2, 6, 3], P('wide', 'narrow'), may hold values from 0 to 7, as said below
- send_rows: int32 [16, 2, 4, 64], P('wide', 'narrow'), may hold values from 0 to 767, as said below
- cov_plane: bfloat16 [192, 192], replicated, may hold values from -0.4375 to 0.4375
- cov_vert: bfloat16 [128, 128], replicated, may hold values from -0.5 to 0.5
Outputs:
- adjoint: bfloat16 [16, 2, 768, 256], P('wide', 'narrow')
- smoothed: bfloat16 [16, 2, 768, 256], P('wide', 'narrow')
Inputs may be any that keep to these rules, and one draw needn't show every extreme that they name: `block_cols`: entry 0 of every block row's list is that block row itself; subdomain blocks are numbered with the own blocks first, then the margin. `send_rows`: the 256 entries of one device are distinct and include rows 0 and 767.
All inputs are finite; a program needn't handle non-finite values.
Results may differ from a plain program's by a relative error of at most 0.0085.
Values may be sent and summed in bfloat16 or wider, within the bound.
No kernel may reach another device: no remote copies, remote signals or barrier semaphores. Data moves between devices by JAX's collectives and lax.ppermute only.
A program may use at most 64 MiB of HBM per device.

v0:
```python
import functools

import jax
import jax.numpy as jnp
from jax import lax
from jax.experimental import pallas as pl
from jax.experimental.pallas import tpu as pltpu
from jax.sharding import PartitionSpec as P

ZL = 64
SWEEPS = 4
LANES = 128
SELECT_FLOPS = 6 * 10 ** 8
PICK_FLOPS = 2 * 10 ** 9
BF = jnp.bfloat16
F32 = jnp.float32
VM = pl.BlockSpec(memory_space=pltpu.VMEM)
ANY = pl.BlockSpec(memory_space=pl.ANY)


def wide_slot(w, n, parity):
    return (w & 1) ^ parity ^ 1


def narrow_slot(w, n, parity):
    return 2 + ((n & 1) ^ parity ^ 1)


def mixed_slot(w, n, kind):
    turn = (w ^ (w >> 1) ^ kind) & 1
    return (1 - turn) * wide_slot(w, n, 1) + turn * narrow_slot(w, n, 0)


def has_partner(w, n, slot, wide, narrow):
    inside = [w > 0, w + 1 < wide, n > 0, n + 1 < narrow]
    return sum((slot == k) * inside[k] for k in range(4))


def matchings():
    wide, narrow = lax.axis_size("wide"), lax.axis_size("narrow")
    if narrow == 2 and wide % 4 == 0:
        rules = [(mixed_slot, 0), (mixed_slot, 1), (wide_slot, 0)]
    else:
        rules = [(wide_slot, 1)] * (wide > 2) + [(narrow_slot, 1)] * (narrow > 2)
        rules += [(narrow_slot, 0)] * (narrow > 1) + [(wide_slot, 0)] * (wide > 1)
    found = []
    for rule, kind in rules:
        pairs = []
        for w in range(wide):
            for n in range(narrow):
                slot = rule(w, n, kind)
                if has_partner(w, n, slot, wide, narrow):
                    step = ((-1, 0), (1, 0), (0, -1), (0, 1))[slot]
                    target = (w + step[0], n + step[1])
                elif slot < 2:
                    target = (w, n ^ 1 if n ^ 1 < narrow else n)
                else:
                    target = (w ^ 1 if w ^ 1 < wide else w, n)
                pairs.append((w * narrow + n, target[0] * narrow + target[1]))
        found.append((rule, kind, tuple(pairs)))
    return found


def own_slots(found):
    w, n = lax.axis_index("wide"), lax.axis_index("narrow")
    wide, narrow = lax.axis_size("wide"), lax.axis_size("narrow")
    slots = [rule(w, n, kind) for rule, kind, _ in found]
    return [(slot, has_partner(w, n, slot, wide, narrow) == 1) for slot in slots]


def swap(messages, found):
    return [lax.ppermute(m, ("wide", "narrow"), list(f[-1])) for m, f in zip(messages, found)]


def mm(a, b):
    return jnp.dot(a, b, preferred_element_type=F32)


def mm_t(a, b):
    return lax.dot_general(a, b, (((1,), (1,)), ((), ())), preferred_element_type=F32)


def iota(shape, dim):
    return lax.broadcasted_iota(jnp.int32, shape, dim)


def call(body, outs, args, scratch=(), specs=None, flops=0, limit=8, out_specs=None):
    size = sum(a.size * a.dtype.itemsize for a in args)
    return pl.pallas_call(
        body,
        out_shape=outs,
        in_specs=specs or [VM] * len(args),
        out_specs=out_specs or [VM] * len(outs),
        scratch_shapes=list(scratch),
        compiler_params=pltpu.CompilerParams(vmem_limit_bytes=limit * 1024 * 1024),
        cost_estimate=pl.CostEstimate(flops=flops, bytes_accessed=size, transcendentals=0),
    )(*args)


def join_halo(got):
    pieces = [piece[...] for piece in got]
    return jnp.concatenate(pieces + [jnp.zeros_like(pieces[0])] * (4 - len(pieces)), axis=0)


def send(messages, values):
    width = messages[0].shape[0]
    for m, message in enumerate(messages):
        message[...] = values[m * width:(m + 1) * width, :].astype(BF)


def keep_split(high_ref, low_ref, rows, value):
    high = value.astype(BF)
    high_ref[rows] = high
    low_ref[rows] = (value - high.astype(F32)).astype(BF)


def select_body(found, own, send_ref, select_ref):
    width = send_ref.shape[1]
    diagonal = iota((width, width), 0) == iota((width, width), 1)
    pieces = []
    for slot, paired in own_slots(found):
        rows = jnp.where(paired, send_ref[pl.ds(slot, 1), :], -1).astype(F32)
        pieces.append(jnp.where(diagonal, rows, 0.0))
    column = jnp.sum(jnp.concatenate(pieces, axis=0), axis=1, keepdims=True).astype(jnp.int32)
    select_ref[...] = (iota((len(found) * width, own), 1) == column).astype(F32).astype(BF)


def pick_body(select_ref, rhs_ref, *messages):
    send(messages, mm(select_ref[...], rhs_ref[...]))


def setup_body(found, width, cols_ref, inverse_ref, blocks_ref, rhs_ref, select_ref, *rest):
    inverse_halo_ref, blocks_halo_ref, inverse_sent_ref, blocks_sent_ref, state_ref, base_ref = rest[:6]
    high_ref, low_ref = rest[6:]
    own = rhs_ref.shape[0]
    halo = 4 * width
    places = iota((1, halo), 1)
    starts = jnp.full((1, halo), -halo, jnp.int32)
    for m, (slot, _) in enumerate(own_slots(found)):
        here = lax.div(places, width) == m
        starts = jnp.where(here, slot * width + lax.rem(places, width), starts)
    arrange = (iota((halo, halo), 0) == starts).astype(F32).astype(BF)
    rows, links, size, _ = blocks_ref.shape
    for j in range(rows):
        here = slice(j * size, (j + 1) * size)
        columns = [cols_ref[j, k] for k in range(links)]
        for c in range(halo // size):
            total = None
            for k in range(links):
                part = jnp.where(columns[k] == own // size + c, blocks_ref[j, k].astype(F32), 0.0)
                total = part if total is None else total + part
            lanes = slice(c * size, (c + 1) * size)
            keep_split(high_ref, low_ref, (here, lanes), total)
    for part, half_ref in enumerate((high_ref, low_ref)):
        blocks_halo_ref[part] = mm(half_ref[...], arrange).astype(BF)
    step = own // 2
    for i in range(0, own, step):
        here = slice(i, i + step)
        inverse_halo_ref[here, :] = mm(inverse_ref[here, own:], arrange).astype(BF)
        value = mm(inverse_ref[here, :own], rhs_ref[...])
        state_ref[here, :] = value
        keep_split(high_ref, low_ref, here, value)
    inverse_sent_ref[...] = mm(select_ref[...], inverse_halo_ref[...]).astype(BF)
    sent = select_ref.shape[0]
    for part in range(2):
        here = slice(part * sent, (part + 1) * sent)
        blocks_sent_ref[here, :] = mm(select_ref[...], blocks_halo_ref[part]).astype(BF)
    base_ref[...] = mm(select_ref[...], high_ref[...]) + mm(select_ref[...], low_ref[...])


def sent_update_body(count, base_ref, sent_ref, *rest):
    got, messages = rest[:count], rest[count:]
    halo = jnp.concatenate([piece[...] for piece in got], axis=0)
    send(messages, base_ref[...] + mm(sent_ref[:, :halo.shape[0]], halo))


def sent_residual_body(count, turn, base_ref, sent_ref, *rest):
    got, messages = rest[:count], rest[count:]
    halo = jnp.concatenate([piece[...] for piece in got[turn:] + got[:turn]], axis=0)
    part = mm(sent_ref[:, :halo.shape[0]], halo)
    sent = base_ref.shape[0]
    send(messages, base_ref[...] - (part[:sent] + part[sent:]))


def update_body(count, cols_ref, state_ref, inverse_halo_ref, blocks_ref, rhs_ref, select_ref, *rest):
    got, (iterate_ref, part_ref, base_ref, sub_ref, high_ref, low_ref) = rest[:count], rest[count:]
    own = state_ref.shape[0]
    halo = join_halo(got)
    step = own // 2
    for i in range(0, own, step):
        here = slice(i, i + step)
        value = state_ref[here, :] + mm(inverse_halo_ref[here, :], halo)
        iterate_ref[here, :] = value
        sub_ref[here, :] = value.astype(BF)
    sub_ref[own:, :] = jnp.zeros((sub_ref.shape[0] - own, sub_ref.shape[1]), BF)
    rows, links, size, _ = blocks_ref.shape
    for j in range(rows):
        starts = [pl.multiple_of(cols_ref[j, k] * size, size) for k in range(links)]
        values = jnp.concatenate([blocks_ref[j, k] for k in range(links)], axis=1)
        coupled = jnp.concatenate([sub_ref[pl.ds(start, size), :] for start in starts], axis=0)
        total = mm(values, coupled)
        here = slice(j * size, (j + 1) * size)
        value = rhs_ref[here, :].astype(F32) - total
        part_ref[here, :] = value
        keep_split(high_ref, low_ref, here, value)
    base_ref[...] = mm(select_ref[...], high_ref[...]) + mm(select_ref[...], low_ref[...])


def residual_body(count, turn, part_ref, blocks_halo_ref, iterate_ref, inverse_ref, select_ref, *rest):
    got, rest = rest[:count], list(rest[count:])
    state_ref = rest.pop(0)
    resid_ref, *split = rest[-3:] if len(rest) == 4 else rest
    own = part_ref.shape[0]
    halo = join_halo(got[turn:] + got[:turn])
    step = own // 2
    for i in range(0, own, step):
        here = slice(i, i + step)
        outer = mm(blocks_halo_ref[0, here, :], halo) + mm(blocks_halo_ref[1, here, :], halo)
        resid_ref[here, :] = (part_ref[here, :] - outer).astype(BF)
    for i in range(0, own, step):
        here = slice(i, i + step)
        value = iterate_ref[here, :] + mm(inverse_ref[here, :own], resid_ref[...])
        state_ref[here, :] = value
        if split:
            keep_split(*split, here, value)
    if split:
        rest[0][...] = mm(select_ref[...], split[0][...]) + mm(select_ref[...], split[1][...])


def last_update_body(count, state_ref, inverse_halo_ref, *rest):
    got, (round_ref,) = rest[:count], rest[count:]
    halo = join_halo(got)
    step = state_ref.shape[0] // 2
    for i in range(0, state_ref.shape[0], step):
        here = slice(i, i + step)
        round_ref[here, :] = (state_ref[here, :] + mm(inverse_halo_ref[here, :], halo)).astype(BF)


def turn_body(state_ref, order_ref, turned_ref):
    value = state_ref[...]
    high = value.astype(BF)
    low = (value - high.astype(F32)).astype(BF)
    columns = value.shape[1]
    both = mm(jnp.concatenate([high, low], axis=1).T, order_ref[...])
    turned_ref[...] = both[:columns] + both[columns:]


def wire_body(count, turned_ref, halo_table_ref, *rest):
    got, (wire_ref,) = rest[:count], rest[count:]
    wire_ref[...] = (turned_ref[...] + mm(join_halo(got).T, halo_table_ref[...])).astype(BF)


def one_hot(rows_of, shape):
    return (iota(shape, 0) == rows_of(iota((1, shape[1]), 1))).astype(F32).astype(BF)


def order_body(inverse_halo_ref, order_ref, halo_table_ref):
    own = order_ref.shape[0]
    tile = own // ZL
    order_ref[...] = one_hot(lambda k: lax.rem(k, ZL) * tile + lax.div(k, ZL), (own, own))
    halo_table_ref[...] = mm(inverse_halo_ref[...].T, order_ref[...]).astype(BF)


def tables_body(wide, narrow, cov_plane_ref, cov_vert_ref, plane_ref, spread_ref, vert_ref):
    plane = plane_ref.shape[0]
    tile = plane // wide
    turn = one_hot(lambda k: lax.rem(k, wide) * tile + lax.div(k, wide), (plane, plane))
    half = mm(cov_plane_ref[...], turn).astype(BF)
    plane_ref[...] = mm(half.T, turn).astype(BF).T
    share = LANES // ZL
    depth = narrow * ZL
    width = narrow * LANES

    def source(k):
        e, n, l = lax.div(k, depth), lax.rem(lax.div(k, ZL), narrow), lax.rem(k, ZL)
        return n * LANES + e * ZL + l

    spread = one_hot(source, (width, width))
    spread_ref[...] = spread
    turned = cov_vert_ref[...].astype(F32).T
    zero = jnp.zeros_like(turned)
    blocks = jnp.concatenate(
        [jnp.concatenate([turned if i == e else zero for i in range(share)], axis=1) for e in range(share)],
        axis=0,
    ).astype(BF)
    vert_ref[...] = mm_t(blocks, spread).astype(BF)


def mix_body(wide, narrow, group, in_ref, plane_ref, spread_ref, vert_ref, state_ref, inverse_halo_ref, *rest):
    got, (out_ref, adjoint_hbm, cells_ref, flat_ref, wire_ref, round_ref, sem) = rest[:-7], rest[-7:]
    last_update_body(len(got), state_ref, inverse_halo_ref, *got, round_ref)
    keep = pltpu.make_async_copy(round_ref, adjoint_hbm, sem)
    keep.start()
    own = in_ref.shape[1]
    tile = own // ZL
    share = LANES // ZL
    depth = narrow * ZL
    block = wide * group
    for g in range(tile // share):
        lanes = slice(g * LANES, (g + 1) * LANES)
        joined = jnp.concatenate([in_ref[n * block:(n + 1) * block, lanes] for n in range(narrow)], axis=1)
        spread = mm(joined, spread_ref[...])
        for e in range(share):
            cells_ref[g * share + e, :block, :] = spread[:, e * depth:(e + 1) * depth]
    for r in range(group):
        for c in range(tile):
            flat_ref[c * wide:(c + 1) * wide, r * depth:(r + 1) * depth] = cells_ref[
                c, pl.ds(r, wide, stride=group), :
            ].astype(BF)
    planar = mm(plane_ref[...], flat_ref[...]).astype(BF)
    for g in range(tile // share):
        stacked = jnp.concatenate(
            [
                jnp.concatenate(
                    [
                        planar[c * wide:(c + 1) * wide, r * depth:(r + 1) * depth]
                        for c in range(g * share, (g + 1) * share)
                    ],
                    axis=1,
                )
                for r in range(group)
            ],
            axis=0,
        )
        mixed = mm(stacked, vert_ref[...])
        for r in range(group):
            for n in range(narrow):
                wire_ref[g, pl.ds(n * block + r, wide, stride=group), :] = mixed[
                    r * wide:(r + 1) * wide, n * LANES:(n + 1) * LANES
                ]
        out_ref[:, g * LANES:(g + 1) * LANES] = wire_ref[g, :narrow * block, :].astype(BF)
    keep.wait()


def unwire_body(in_ref, out_hbm, out_ref, sems):
    own = out_ref.shape[0]
    tile = own // ZL
    runs = sems.shape[0]
    run = ZL // runs
    step = run * tile
    small = one_hot(lambda k: lax.rem(k, run) * tile + lax.div(k, run), (step, step))
    turned = in_ref[...].T
    copies = []
    for b in range(runs):
        here = pl.ds(b * step, step)
        piece = jnp.concatenate([turned[c * ZL + b * run:c * ZL + (b + 1) * run] for c in range(tile)], axis=0)
        out_ref[here, :] = mm(small, piece).astype(BF)
        copy = pltpu.make_async_copy(out_ref.at[here], out_hbm.at[here], sems.at[b])
        copy.start()
        copies.append(copy)
    for copy in copies:
        copy.wait()


def column_tables(inverse_halo, cov_plane, cov_vert):
    own, halo = inverse_halo.shape
    wide, narrow = lax.axis_size("wide"), lax.axis_size("narrow")
    width = narrow * LANES
    plane = cov_plane.shape[0]
    shape = jax.ShapeDtypeStruct
    order = call(order_body, [shape((own, own), BF), shape((halo, own), BF)], [inverse_halo])
    rest = call(
        functools.partial(tables_body, wide, narrow),
        [shape((plane, plane), BF), shape((width, width), BF), shape((width, width), BF)],
        [cov_plane, cov_vert],
    )
    return [tuple(order), tuple(rest)]


def smooth_by_columns(state, inverse_halo, got, tables):
    wide, narrow = lax.axis_size("wide"), lax.axis_size("narrow")
    own, columns = state.shape
    devices = wide * narrow
    group = columns // devices
    depth = narrow * ZL
    tile = own // ZL
    shape = jax.ShapeDtypeStruct
    (order, halo_table), (plane_mix, spread, vert_mix) = tables
    (turned,) = call(turn_body, [shape((columns, own), F32)], [state, order])
    (wire,) = call(functools.partial(wire_body, len(got)), [shape((columns, own), BF)], [turned, halo_table, *got])
    there = lax.all_to_all(
        wire.reshape(devices, group, own), ("narrow", "wide"), split_axis=0, concat_axis=0, tiled=True
    )
    mixed, adjoint = call(
        functools.partial(mix_body, wide, narrow, group),
        [shape((columns, own), BF), shape((own, columns), BF)],
        [there.reshape(columns, own), plane_mix, spread, vert_mix, state, inverse_halo, *got],
        [
            pltpu.VMEM((tile, wide * group + group, depth), F32),
            pltpu.VMEM((plane_mix.shape[0], group * depth), BF),
            pltpu.VMEM((own // LANES, columns + group, LANES), F32),
            pltpu.VMEM((own, columns), BF),
            pltpu.SemaphoreType.DMA,
        ],
        out_specs=[VM, ANY],
    )
    back = lax.all_to_all(
        mixed.reshape(devices, group, own), ("narrow", "wide"), split_axis=0, concat_axis=0, tiled=True
    )
    (smoothed,) = call(
        unwire_body,
        [shape((own, columns), BF)],
        [back.reshape(columns, own)],
        [pltpu.VMEM((own, columns), BF), pltpu.SemaphoreType.DMA((4,))],
        out_specs=[ANY],
    )
    return adjoint, smoothed


def smooth_by_layers(adjoint, cov_plane, cov_vert):
    own, columns = adjoint.shape
    layered = adjoint.reshape(ZL, own // ZL, -1)
    planar = jnp.einsum(
        "pq,lqr->lpr",
        cov_plane,
        lax.all_to_all(layered, "wide", split_axis=0, concat_axis=1, tiled=True),
        preferred_element_type=F32,
    ).astype(BF)
    restored = lax.all_to_all(planar, "wide", split_axis=1, concat_axis=0, tiled=True)
    slab_weights = lax.dynamic_slice_in_dim(cov_vert, lax.axis_index("narrow") * ZL, ZL, 0)
    summed = jnp.dot(
        slab_weights,
        lax.all_gather(restored.reshape(ZL, -1), "narrow", axis=0, tiled=True),
        preferred_element_type=F32,
    )
    return summed.astype(BF).reshape(own, -1)


def shards(adjoint_rhs, inverse_rows, blocks, block_cols, send_rows, cov_plane, cov_vert):
    rhs = adjoint_rhs[0, 0]
    inverse = inverse_rows[0, 0]
    block_values = blocks[0, 0]
    cols = block_cols[0, 0]
    send_index = send_rows[0, 0]
    own, columns = rhs.shape
    width = send_index.shape[1]
    halo = 4 * width
    wide, narrow = lax.axis_size("wide"), lax.axis_size("narrow")
    group = columns // (wide * narrow)
    by_columns = columns % (wide * narrow) == 0 and group % 8 == 0 and narrow * ZL == LANES and wide % 16 == 0
    found = matchings()
    count = len(found)
    sent = count * width
    shape = jax.ShapeDtypeStruct
    notes = [shape((width, columns), BF)] * count
    full = shape((own, columns), F32)
    base_shape = shape((sent, columns), F32)
    cell_space = pltpu.VMEM((own, columns), BF)
    (select,) = call(
        functools.partial(select_body, found, own),
        [shape((sent, own), BF)],
        [send_index],
        flops=SELECT_FLOPS,
    )
    messages = call(pick_body, notes, [select, rhs], flops=PICK_FLOPS)
    got = swap(messages, found)
    inverse_halo, blocks_halo, inverse_sent, blocks_sent, state, base = call(
        functools.partial(setup_body, found, width),
        [
            shape((own, halo), BF),
            shape((2, own, halo), BF),
            shape((sent, halo), BF),
            shape((2 * sent, halo), BF),
            full,
            base_shape,
        ],
        [cols, inverse, block_values, rhs, select],
        [cell_space, cell_space],
        limit=12,
    )
    tables = column_tables(inverse_halo, cov_plane, cov_vert) if by_columns else []
    for sweep in range(SWEEPS - 1):
        messages = call(
            functools.partial(sent_update_body, count), notes, [base, inverse_sent, *got], limit=4
        )
        arrived, got = got, swap(messages, found)
        iterate, part, base = call(
            functools.partial(update_body, count),
            [full, full, base_shape],
            [cols, state, inverse_halo, block_values, rhs, select, *arrived],
            [pltpu.VMEM((own + halo, columns), BF), cell_space, cell_space],
        )
        turn = 1 if sweep == 1 and count == 3 else 0
        arrived = got[count - turn:] + got[:count - turn]
        messages = call(
            functools.partial(sent_residual_body, count, turn),
            notes,
            [base, blocks_sent, *arrived],
            limit=4,
        )
        got = swap(messages, found)
        if sweep < len(tables):
            tables[sweep], part = lax.optimization_barrier((tables[sweep], part))
        more = sweep < SWEEPS - 2
        state, *bases = call(
            functools.partial(residual_body, count, turn),
            [full] + [base_shape] * more,
            [part, blocks_halo, iterate, inverse, select, *arrived],
            [cell_space] * (1 + 2 * more),
        )
        base = bases[0] if more else None
    if by_columns:
        adjoint, smoothed = smooth_by_columns(state, inverse_halo, got, tables)
    else:
        cells = shape((own, columns), BF)
        (adjoint,) = call(functools.partial(last_update_body, count), [cells], [state, inverse_halo, *got])
        smoothed = smooth_by_layers(adjoint, cov_plane, cov_vert)
    return (adjoint[None, None], smoothed[None, None])


def solution(mesh):
    in_specs = (
        P("wide", "narrow", None, None),
        P("wide", "narrow", None, None),
        P("wide", "narrow", None, None, None, None),
        P("wide", "narrow", None, None),
        P("wide", "narrow", None, None),
        P(),
        P(),
    )
    out_specs = (P("wide", "narrow", None, None), P("wide", "narrow", None, None))
    return jax.shard_map(shards, mesh=mesh, in_specs=in_specs, out_specs=out_specs, check_vma=False)
```

profile of v0, /device:TPU:0, one launch (start us, length us, event | category | flops | bytes accessed | tf_op | source)
XLA Modules:
  0.0 73.2 jit_solution(1784899844616191166)
XLA Ops:
  0.6 0.7 copy-done.5
  1.9 3.0 %collective-permute-start = (bf16[64,256]{1,0:T(8,128)(2,1)S(1)}, bf16[64,256]{1,0:T(8,128)(2,1)S(1)}, u32[]{:S(2)}, u32[]{:S(2)}) collective-permute-start(bf16[64,256]{1,0:T(8,128)(2,1)S(1)} %get-tuple-element.63), channel_id=1, source_target_pairs={{0,1},{1,0},{2,3},{3,2},{4,5},{5,4},{6,8},{7,9},{8,6},{9,7},{10,11... | collective-permute-start | bytes 98312 | tf_op jit(solution)/shard_map/ppermute | solution.py:72
  5.0 1.6 %collective-permute-start.2 = (bf16[64,256]{1,0:T(8,128)(2,1)S(1)}, bf16[64,256]{1,0:T(8,128)(2,1)S(1)}, u32[]{:S(2)}, u32[]{:S(2)}) collective-permute-start(bf16[64,256]{1,0:T(8,128)(2,1)S(1)} %get-tuple-element.65), channel_id=1, source_target_pairs={{0,2},{1,3},{2,0},{3,1},{4,6},{5,7},{6,4},{7,5},{8,10},{9,11},{10,... | collective-permute-start | bytes 98312 | tf_op jit(solution)/shard_map/ppermute | solution.py:72
  6.6 1.6 %shard_map.88 = (bf16[768,256]{1,0:T(8,128)(2,1)S(1)}, bf16[2,768,256]{2,1,0:T(8,128)(2,1)S(1)}, bf16[192,256]{1,0:T(8,128)(2,1)S(1)}, bf16[384,256]{1,0:T(8,128...) custom-call(s32[6,3]{1,0:T(8,128)S(1)} %bitcast.28, bf16[768,1024]{1,0:T(8,128)(2,1)S(1)} %bitcast.11, ...), custom_call_target="tpu_custom_call" | custom-call | bytes 2850888 | tf_op jit(solution)/shard_map/pallas_call | solution.py:89
  8.2 0.6 collective-permute-done.1.rest_1_
  9.4 1.7 %collective-permute-start.4 = (bf16[64,256]{1,0:T(8,128)(2,1)S(1)}, bf16[64,256]{1,0:T(8,128)(2,1)S(1)}, u32[]{:S(2)}, u32[]{:S(2)}) collective-permute-start(bf16[64,256]{1,0:T(8,128)(2,1)S(1)} %get-tuple-element.73), channel_id=1, source_target_pairs={{0,1},{1,0},{2,4},{3,5},{4,2},{5,3},{6,7},{7,6},{8,9},{9,8},{10,12... | collective-permute-start | bytes 98312 | tf_op jit(solution)/shard_map/ppermute | solution.py:72
  11.1 1.1 %shard_map.91 = (f32[768,256]{1,0:T(8,128)S(1)}, f32[768,256]{1,0:T(8,128)S(1)}, f32[192,256]{1,0:T(8,128)S(1)}) custom-call(s32[6,3]{1,0:T(8,128)S(1)} %bitcast.29, f32[768,256]{1,0:T(8,128)S(1)} %get-tuple-element.62.state_ref, bf16[768,256]{1,0:T(8,128)(2,1)S(1)} %get-tuple-element.59.inverse_halo_ref, bf16[6,3,128,128]{3,2,1,0:T(8,128)(2,1)S(1)} %bitcast.16, ...), custom_call_target="tpu_custom_call" | custom-call | bytes 2555976 | tf_op jit(solution)/shard_map/pallas_call | solution.py:89
  12.2 0.8 %collective-permute-done.3.rest_0_ = bf16[64,256]{1,0:T(8,128)(2,1)S(1)} collective-permute-done((bf16[64,256]{1,0:T(8,128)(2,1)S(1)}, bf16[64,256]{1,0:T(8,128)(2,1)S(1)}, u32[]{:S(2)}, u32[]{:S(2)}) %collective-permute-start.3) | collective-permute-done | bytes 32800 | tf_op jit(solution)/shard_map/ppermute | solution.py:72
  13.5 1.7 %collective-permute-start.6 = (bf16[64,256]{1,0:T(8,128)(2,1)S(1)}, bf16[64,256]{1,0:T(8,128)(2,1)S(1)}, u32[]{:S(2)}, u32[]{:S(2)}) collective-permute-start(bf16[64,256]{1,0:T(8,128)(2,1)S(1)} %get-tuple-element.78), channel_id=1, source_target_pairs={{0,1},{1,0},{2,3},{3,2},{4,5},{5,4},{6,8},{7,9},{8,6},{9,7},{10,11... | collective-permute-start | bytes 98312 | tf_op jit(solution)/shard_map/ppermute | solution.py:72
  15.6 0.5 collective-permute-start.8
  16.1 0.7 shard_map.89
  16.8 1.2 %shard_map.93 = (f32[768,256]{1,0:T(8,128)S(1)}, f32[192,256]{1,0:T(8,128)S(1)}) custom-call(f32[768,256]{1,0:T(8,128)S(1)} %get-tuple-element.67.part_ref, bf16[2,768,256]{2,1,0:T(8,128)(2,1)S(1)} %get-tuple-element.68.blocks_halo_ref, f32[768,256]{1,0:T(8,128)S(1)} %get-tuple-element.69.iterate_ref, bf16[768,1024]{1,0:T(8,128)(2,1)S(1)} %bitcast.12, ...), custom_call_target="tpu_custom_call" | custom-call | bytes 4325376 | tf_op jit(solution)/shard_map/pallas_call | solution.py:89
  18.0 1.2 %collective-permute-done.7.rest_1_ = bf16[64,256]{1,0:T(8,128)(2,1)S(1)} collective-permute-done((bf16[64,256]{1,0:T(8,128)(2,1)S(1)}, bf16[64,256]{1,0:T(8,128)(2,1)S(1)}, u32[]{:S(2)}, u32[]{:S(2)}) %collective-permute-start.7) | collective-permute-done | bytes 32800 | tf_op jit(solution)/shard_map/ppermute | solution.py:72
  19.4 0.4 collective-permute-start.10
  19.8 1.7 %collective-permute-start.11 = (bf16[64,256]{1,0:T(8,128)(2,1)S(1)}, bf16[64,256]{1,0:T(8,128)(2,1)S(1)}, u32[]{:S(2)}, u32[]{:S(2)}) collective-permute-start(bf16[64,256]{1,0:T(8,128)(2,1)S(1)} %get-tuple-element.87), channel_id=1, source_target_pairs={{0,1},{1,0},{2,4},{3,5},{4,2},{5,3},{6,7},{7,6},{8,9},{9,8},{10,12... | collective-permute-start | bytes 98312 | tf_op jit(solution)/shard_map/ppermute | solution.py:72
  21.5 1.1 %shard_map.95 = (f32[768,256]{1,0:T(8,128)S(1)}, f32[768,256]{1,0:T(8,128)S(1)}, f32[192,256]{1,0:T(8,128)S(1)}) custom-call(s32[6,3]{1,0:T(8,128)S(1)} %bitcast.30, f32[768,256]{1,0:T(8,128)S(1)} %get-tuple-element.75.state_ref, bf16[768,256]{1,0:T(8,128)(2,1)S(1)} %get-tuple-element.59.inverse_halo_ref, bf16[6,3,128,128]{3,2,1,0:T(8,128)(2,1)S(1)} %bitcast.17, ...), custom_call_target="tpu_custom_call" | custom-call | bytes 2555976 | tf_op jit(solution)/shard_map/pallas_call | solution.py:89
  22.6 0.8 %collective-permute-done.10.rest_1_ = bf16[64,256]{1,0:T(8,128)(2,1)S(1)} collective-permute-done((bf16[64,256]{1,0:T(8,128)(2,1)S(1)}, bf16[64,256]{1,0:T(8,128)(2,1)S(1)}, u32[]{:S(2)}, u32[]{:S(2)}) %collective-permute-start.10) | collective-permute-done | bytes 32800 | tf_op jit(solution)/shard_map/ppermute | solution.py:72
  23.9 1.7 %collective-permute-start.12 = (bf16[64,256]{1,0:T(8,128)(2,1)S(1)}, bf16[64,256]{1,0:T(8,128)(2,1)S(1)}, u32[]{:S(2)}, u32[]{:S(2)}) collective-permute-start(bf16[64,256]{1,0:T(8,128)(2,1)S(1)} %get-tuple-element.90), channel_id=1, source_target_pairs={{0,1},{1,0},{2,3},{3,2},{4,5},{5,4},{6,8},{7,9},{8,6},{9,7},{10,11... | collective-permute-start | bytes 98312 | tf_op jit(solution)/shard_map/ppermute | solution.py:72
  26.0 0.5 shard_map.86
  26.5 1.2 %shard_map.97 = (f32[768,256]{1,0:T(8,128)S(1)}, f32[192,256]{1,0:T(8,128)S(1)}) custom-call(f32[768,256]{1,0:T(8,128)S(1)} %get-tuple-element.82.part_ref, bf16[2,768,256]{2,1,0:T(8,128)(2,1)S(1)} %get-tuple-element.68.blocks_halo_ref, f32[768,256]{1,0:T(8,128)S(1)} %get-tuple-element.83.iterate_ref, bf16[768,1024]{1,0:T(8,128)(2,1)S(1)} %bitcast.13, ...), custom_call_target="tpu_custom_call" | custom-call | bytes 4325376 | tf_op jit(solution)/shard_map/pallas_call | solution.py:89
  27.9 1.7 %collective-permute-done.13.rest_1_ = bf16[64,256]{1,0:T(8,128)(2,1)S(1)} collective-permute-done((bf16[64,256]{1,0:T(8,128)(2,1)S(1)}, bf16[64,256]{1,0:T(8,128)(2,1)S(1)}, u32[]{:S(2)}, u32[]{:S(2)}) %collective-permute-start.13) | collective-permute-done | bytes 32800 | tf_op jit(solution)/shard_map/ppermute | solution.py:72
  30.2 1.7 %collective-permute-start.16 = (bf16[64,256]{1,0:T(8,128)(2,1)S(1)}, bf16[64,256]{1,0:T(8,128)(2,1)S(1)}, u32[]{:S(2)}, u32[]{:S(2)}) collective-permute-start(bf16[64,256]{1,0:T(8,128)(2,1)S(1)} %get-tuple-element.97), channel_id=1, source_target_pairs={{0,1},{1,0},{2,4},{3,5},{4,2},{5,3},{6,7},{7,6},{8,9},{9,8},{10,12... | collective-permute-start | bytes 98312 | tf_op jit(solution)/shard_map/ppermute | solution.py:72
  31.9 1.1 %shard_map.99 = (f32[768,256]{1,0:T(8,128)S(1)}, f32[768,256]{1,0:T(8,128)S(1)}, f32[192,256]{1,0:T(8,128)S(1)}) custom-call(s32[6,3]{1,0:T(8,128)S(1)} %bitcast.31, f32[768,256]{1,0:T(8,128)S(1)} %get-tuple-element.88.state_ref, bf16[768,256]{1,0:T(8,128)(2,1)S(1)} %get-tuple-element.59.inverse_halo_ref, bf16[6,3,128,128]{3,2,1,0:T(8,128)(2,1)S(1)} %bitcast.18, ...), custom_call_target="tpu_custom_call" | custom-call | bytes 2555976 | tf_op jit(solution)/shard_map/pallas_call | solution.py:89
  33.0 0.8 %collective-permute-done.15.rest_0_ = bf16[64,256]{1,0:T(8,128)(2,1)S(1)} collective-permute-done((bf16[64,256]{1,0:T(8,128)(2,1)S(1)}, bf16[64,256]{1,0:T(8,128)(2,1)S(1)}, u32[]{:S(2)}, u32[]{:S(2)}) %collective-permute-start.15) | collective-permute-done | bytes 32800 | tf_op jit(solution)/shard_map/ppermute | solution.py:72
  34.3 1.7 %collective-permute-start.18 = (bf16[64,256]{1,0:T(8,128)(2,1)S(1)}, bf16[64,256]{1,0:T(8,128)(2,1)S(1)}, u32[]{:S(2)}, u32[]{:S(2)}) collective-permute-start(bf16[64,256]{1,0:T(8,128)(2,1)S(1)} %get-tuple-element.102), channel_id=1, source_target_pairs={{0,1},{1,0},{2,3},{3,2},{4,5},{5,4},{6,8},{7,9},{8,6},{9,7},{10,11... | collective-permute-start | bytes 98312 | tf_op jit(solution)/shard_map/ppermute | solution.py:72
  36.4 0.8 %shard_map.101.state_ref = f32[768,256]{1,0:T(8,128)S(1)} custom-call(f32[768,256]{1,0:T(8,128)S(1)} %get-tuple-element.93.part_ref, bf16[2,768,256]{2,1,0:T(8,128)(2,1)S(1)} %get-tuple-element.68.blocks_halo_ref, f32[768,256]{1,0:T(8,128)S(1)} %get-tuple-element.94.iterate_ref, bf16[768,1024]{1,0:T(8,128)(2,1)S(1)} %bitcast.14, ...), custom_call_target="tpu_custom_call" | custom-call | bytes 4325376 | tf_op jit(solution)/shard_map/pallas_call | solution.py:89
  37.2 0.8 %shard_map.102.turned_ref = f32[256,768]{1,0:T(8,128)S(1)} custom-call(f32[768,256]{1,0:T(8,128)S(1)} %shard_map.101.state_ref, bf16[768,768]{1,0:T(8,128)(2,1)S(1)} %get-tuple-element.99.order_ref), custom_call_target="tpu_custom_call" | custom-call | bytes 1966080 | tf_op jit(solution)/shard_map/pallas_call | solution.py:89
  38.3 1.7 %collective-permute-done.19.rest_1_ = bf16[64,256]{1,0:T(8,128)(2,1)S(1)} collective-permute-done((bf16[64,256]{1,0:T(8,128)(2,1)S(1)}, bf16[64,256]{1,0:T(8,128)(2,1)S(1)}, u32[]{:S(2)}, u32[]{:S(2)}) %collective-permute-start.19) | collective-permute-done | bytes 32800 | tf_op jit(solution)/shard_map/ppermute | solution.py:72
  40.3 15.6 %all_to_all.10 = bf16[32,8,768]{2,1,0:T(8,128)(2,1)S(1)} all-to-all(bf16[32,8,768]{2,1,0:T(8,128)(2,1)S(1)} %bitcast.25), channel_id=1, replica_groups=mesh['wide'=16,'narrow'=2] {'narrow','wide'}, dimensions={0} | all-to-all | bytes 786432 | tf_op jit(solution)/shard_map/all_to_all | solution.py:381
  55.8 1.0 %shard_map.105 = (bf16[256,768]{1,0:T(8,128)(2,1)S(1)}, bf16[768,256]{1,0:T(8,128)(2,1)}) custom-call(bf16[256,768]{1,0:T(8,128)(2,1)S(1)} %bitcast.26, bf16[192,192]{1,0:T(8,128)(2,1)S(1)} %get-tuple-element.105.plane_ref, bf16[256,256]{1,0:T(8,128)(2,1)S(1)} %get-tuple-element.106.spread_ref, bf16[256,256]{1,0:T(8,128)(2,1)S(1)} %get-tuple-element.107.vert_ref, ...), custom_call_target="tpu_custom_call" | custom-call | bytes 2007040 | tf_op jit(solution)/shard_map/pallas_call | solution.py:89
  56.9 15.2 %all_to_all.11 = bf16[32,8,768]{2,1,0:T(8,128)(2,1)S(1)} all-to-all(bf16[32,8,768]{2,1,0:T(8,128)(2,1)S(1)} %bitcast.27), channel_id=1, replica_groups=mesh['wide'=16,'narrow'=2] {'narrow','wide'}, dimensions={0} | all-to-all | bytes 786432 | tf_op jit(solution)/shard_map/all_to_all | solution.py:397
  72.1 1.1 %shard_map.106 = bf16[768,256]{1,0:T(8,128)(2,1)} custom-call(bf16[256,768]{1,0:T(8,128)(2,1)S(1)} %bitcast.24), custom_call_target="tpu_custom_call" | custom-call | bytes 393216 | tf_op jit(solution)/shard_map/pallas_call | solution.py:89
  (48 shorter events, 5.6 us)
Async XLA Ops:
  0.6 1.0 %copy-start.2 = (bf16[1,1,768,256]{3,2,1,0:T(8,128)(2,1)S(1)}, bf16[1,1,768,256]{3,2,1,0:T(8,128)(2,1)}, u32[]{:S(2)}) copy-start(bf16[1,1,768,256]{3,2,1,0:T(8,128)(2,1)} %param.7) | copy-start | bytes 1179652
  0.6 0.7 %copy-start.5 = (s32[1,1,4,64]{3,2,1,0:T(4,128)S(1)}, s32[1,1,4,64]{3,2,1,0:T(4,128)}, u32[]{:S(2)}) copy-start(s32[1,1,4,64]{3,2,1,0:T(4,128)} %param.11) | copy-start | bytes 3076
  1.6 4.9 %copy-start.6 = (s32[1,1,6,3]{2,1,3,0:T(1,128)S(1)}, s32[1,1,6,3]{2,1,3,0:T(1,128)}, u32[]{:S(2)}) copy-start(s32[1,1,6,3]{2,1,3,0:T(1,128)} %param.10) | copy-start | bytes 220
  1.6 5.0 %copy-start = (bf16[1,1,768,1024]{3,2,1,0:T(8,128)(2,1)S(1)}, bf16[1,1,768,1024]{3,2,1,0:T(8,128)(2,1)}, u32[]{:S(2)}) copy-start(bf16[1,1,768,1024]{3,2,1,0:T(8,128)(2,1)} %param.8) | copy-start | bytes 4718596
  1.6 5.0 %copy-start.1 = (bf16[1,1,6,3,128,128]{5,4,3,2,1,0:T(8,128)(2,1)S(1)}, bf16[1,1,6,3,128,128]{5,4,3,2,1,0:T(8,128)(2,1)}, u32[]{:S(2)}) copy-start(bf16[1,1,6,3,128,128]{5,4,3,2,1,0:T(8,128)(2,1)} %param.9) | copy-start | bytes 1769476
  1.9 6.3 %collective-permute-start = (bf16[64,256]{1,0:T(8,128)(2,1)S(1)}, bf16[64,256]{1,0:T(8,128)(2,1)S(1)}, u32[]{:S(2)}, u32[]{:S(2)}) collective-permute-start(bf16[64,256]{1,0:T(8,128)(2,1)S(1)} %get-tuple-element.63), channel_id=1, source_target_pairs={{0,1},{1,0},{2,3},{3,2},{4,5},{5,4},{6,8},{7,9},{8,6},{9,7},{10,11... | collective-permute-start | bytes 98312 | tf_op jit(solution)/shard_map/ppermute | solution.py:72
  4.9 3.9 %collective-permute-start.1 = (bf16[64,256]{1,0:T(8,128)(2,1)S(1)}, bf16[64,256]{1,0:T(8,128)(2,1)S(1)}, u32[]{:S(2)}, u32[]{:S(2)}) collective-permute-start(bf16[64,256]{1,0:T(8,128)(2,1)S(1)} %get-tuple-element.64), channel_id=1, source_target_pairs={{0,1},{1,0},{2,4},{3,5},{4,2},{5,3},{6,7},{7,6},{8,9},{9,8},{10,12... | collective-permute-start | bytes 98312 | tf_op jit(solution)/shard_map/ppermute | solution.py:72
  5.0 3.8 %collective-permute-start.2 = (bf16[64,256]{1,0:T(8,128)(2,1)S(1)}, bf16[64,256]{1,0:T(8,128)(2,1)S(1)}, u32[]{:S(2)}, u32[]{:S(2)}) collective-permute-start(bf16[64,256]{1,0:T(8,128)(2,1)S(1)} %get-tuple-element.65), channel_id=1, source_target_pairs={{0,2},{1,3},{2,0},{3,1},{4,6},{5,7},{6,4},{7,5},{8,10},{9,11},{10,... | collective-permute-start | bytes 98312 | tf_op jit(solution)/shard_map/ppermute | solution.py:72
  9.0 4.0 %collective-permute-start.3 = (bf16[64,256]{1,0:T(8,128)(2,1)S(1)}, bf16[64,256]{1,0:T(8,128)(2,1)S(1)}, u32[]{:S(2)}, u32[]{:S(2)}) collective-permute-start(bf16[64,256]{1,0:T(8,128)(2,1)S(1)} %get-tuple-element.72), channel_id=1, source_target_pairs={{0,1},{1,0},{2,3},{3,2},{4,5},{5,4},{6,8},{7,9},{8,6},{9,7},{10,11... | collective-permute-start | bytes 98312 | tf_op jit(solution)/shard_map/ppermute | solution.py:72
  9.4 3.9 %collective-permute-start.4 = (bf16[64,256]{1,0:T(8,128)(2,1)S(1)}, bf16[64,256]{1,0:T(8,128)(2,1)S(1)}, u32[]{:S(2)}, u32[]{:S(2)}) collective-permute-start(bf16[64,256]{1,0:T(8,128)(2,1)S(1)} %get-tuple-element.73), channel_id=1, source_target_pairs={{0,1},{1,0},{2,4},{3,5},{4,2},{5,3},{6,7},{7,6},{8,9},{9,8},{10,12... | collective-permute-start | bytes 98312 | tf_op jit(solution)/shard_map/ppermute | solution.py:72
  11.1 2.2 %collective-permute-start.5 = (bf16[64,256]{1,0:T(8,128)(2,1)S(1)}, bf16[64,256]{1,0:T(8,128)(2,1)S(1)}, u32[]{:S(2)}, u32[]{:S(2)}) collective-permute-start(bf16[64,256]{1,0:T(8,128)(2,1)S(1)} %get-tuple-element.74), channel_id=1, source_target_pairs={{0,2},{1,3},{2,0},{3,1},{4,6},{5,7},{6,4},{7,5},{8,10},{9,11},{10,... | collective-permute-start | bytes 98312 | tf_op jit(solution)/shard_map/ppermute | solution.py:72
  13.5 4.4 %collective-permute-start.6 = (bf16[64,256]{1,0:T(8,128)(2,1)S(1)}, bf16[64,256]{1,0:T(8,128)(2,1)S(1)}, u32[]{:S(2)}, u32[]{:S(2)}) collective-permute-start(bf16[64,256]{1,0:T(8,128)(2,1)S(1)} %get-tuple-element.78), channel_id=1, source_target_pairs={{0,1},{1,0},{2,3},{3,2},{4,5},{5,4},{6,8},{7,9},{8,6},{9,7},{10,11... | collective-permute-start | bytes 98312 | tf_op jit(solution)/shard_map/ppermute | solution.py:72
  15.3 3.9 %collective-permute-start.7 = (bf16[64,256]{1,0:T(8,128)(2,1)S(1)}, bf16[64,256]{1,0:T(8,128)(2,1)S(1)}, u32[]{:S(2)}, u32[]{:S(2)}) collective-permute-start(bf16[64,256]{1,0:T(8,128)(2,1)S(1)} %get-tuple-element.79), channel_id=1, source_target_pairs={{0,1},{1,0},{2,4},{3,5},{4,2},{5,3},{6,7},{7,6},{8,9},{9,8},{10,12... | collective-permute-start | bytes 98312 | tf_op jit(solution)/shard_map/ppermute | solution.py:72
  15.6 3.6 %collective-permute-start.8 = (bf16[64,256]{1,0:T(8,128)(2,1)S(1)}, bf16[64,256]{1,0:T(8,128)(2,1)S(1)}, u32[]{:S(2)}, u32[]{:S(2)}) collective-permute-start(bf16[64,256]{1,0:T(8,128)(2,1)S(1)} %get-tuple-element.80), channel_id=1, source_target_pairs={{0,2},{1,3},{2,0},{3,1},{4,6},{5,7},{6,4},{7,5},{8,10},{9,11},{10,... | collective-permute-start | bytes 98312 | tf_op jit(solution)/shard_map/ppermute | solution.py:72
  19.4 6.7 %copy-start.3 = (bf16[192,192]{1,0:T(8,128)(2,1)S(1)}, bf16[192,192]{1,0:T(8,128)(2,1)}, u32[]{:S(2)}) copy-start(bf16[192,192]{1,0:T(8,128)(2,1)} %cov_plane_ref.1) | copy-start | bytes 221188
  19.4 6.7 %copy-start.4 = (bf16[128,128]{1,0:T(8,128)(2,1)S(1)}, bf16[128,128]{1,0:T(8,128)(2,1)}, u32[]{:S(2)}) copy-start(bf16[128,128]{1,0:T(8,128)(2,1)} %cov_vert_ref.1) | copy-start | bytes 98308
  19.4 4.0 %collective-permute-start.10 = (bf16[64,256]{1,0:T(8,128)(2,1)S(1)}, bf16[64,256]{1,0:T(8,128)(2,1)S(1)}, u32[]{:S(2)}, u32[]{:S(2)}) collective-permute-start(bf16[64,256]{1,0:T(8,128)(2,1)S(1)} %get-tuple-element.86), channel_id=1, source_target_pairs={{0,1},{1,0},{2,3},{3,2},{4,5},{5,4},{6,8},{7,9},{8,6},{9,7},{10,11... | collective-permute-start | bytes 98312 | tf_op jit(solution)/shard_map/ppermute | solution.py:72
  19.8 3.9 %collective-permute-start.11 = (bf16[64,256]{1,0:T(8,128)(2,1)S(1)}, bf16[64,256]{1,0:T(8,128)(2,1)S(1)}, u32[]{:S(2)}, u32[]{:S(2)}) collective-permute-start(bf16[64,256]{1,0:T(8,128)(2,1)S(1)} %get-tuple-element.87), channel_id=1, source_target_pairs={{0,1},{1,0},{2,4},{3,5},{4,2},{5,3},{6,7},{7,6},{8,9},{9,8},{10,12... | collective-permute-start | bytes 98312 | tf_op jit(solution)/shard_map/ppermute | solution.py:72
  21.5 2.2 %collective-permute-start.9 = (bf16[64,256]{1,0:T(8,128)(2,1)S(1)}, bf16[64,256]{1,0:T(8,128)(2,1)S(1)}, u32[]{:S(2)}, u32[]{:S(2)}) collective-permute-start(bf16[64,256]{1,0:T(8,128)(2,1)S(1)} %get-tuple-element.85), channel_id=1, source_target_pairs={{0,2},{1,3},{2,0},{3,1},{4,6},{5,7},{6,4},{7,5},{8,10},{9,11},{10,... | collective-permute-start | bytes 98312 | tf_op jit(solution)/shard_map/ppermute | solution.py:72
  23.9 4.0 %collective-permute-start.12 = (bf16[64,256]{1,0:T(8,128)(2,1)S(1)}, bf16[64,256]{1,0:T(8,128)(2,1)S(1)}, u32[]{:S(2)}, u32[]{:S(2)}) collective-permute-start(bf16[64,256]{1,0:T(8,128)(2,1)S(1)} %get-tuple-element.90), channel_id=1, source_target_pairs={{0,1},{1,0},{2,3},{3,2},{4,5},{5,4},{6,8},{7,9},{8,6},{9,7},{10,11... | collective-permute-start | bytes 98312 | tf_op jit(solution)/shard_map/ppermute | solution.py:72
  25.7 3.9 %collective-permute-start.13 = (bf16[64,256]{1,0:T(8,128)(2,1)S(1)}, bf16[64,256]{1,0:T(8,128)(2,1)S(1)}, u32[]{:S(2)}, u32[]{:S(2)}) collective-permute-start(bf16[64,256]{1,0:T(8,128)(2,1)S(1)} %get-tuple-element.91), channel_id=1, source_target_pairs={{0,1},{1,0},{2,4},{3,5},{4,2},{5,3},{6,7},{7,6},{8,9},{9,8},{10,12... | collective-permute-start | bytes 98312 | tf_op jit(solution)/shard_map/ppermute | solution.py:72
  26.0 3.6 %collective-permute-start.14 = (bf16[64,256]{1,0:T(8,128)(2,1)S(1)}, bf16[64,256]{1,0:T(8,128)(2,1)S(1)}, u32[]{:S(2)}, u32[]{:S(2)}) collective-permute-start(bf16[64,256]{1,0:T(8,128)(2,1)S(1)} %get-tuple-element.92), channel_id=1, source_target_pairs={{0,2},{1,3},{2,0},{3,1},{4,6},{5,7},{6,4},{7,5},{8,10},{9,11},{10,... | collective-permute-start | bytes 98312 | tf_op jit(solution)/shard_map/ppermute | solution.py:72
  29.8 4.0 %collective-permute-start.15 = (bf16[64,256]{1,0:T(8,128)(2,1)S(1)}, bf16[64,256]{1,0:T(8,128)(2,1)S(1)}, u32[]{:S(2)}, u32[]{:S(2)}) collective-permute-start(bf16[64,256]{1,0:T(8,128)(2,1)S(1)} %get-tuple-element.96), channel_id=1, source_target_pairs={{0,1},{1,0},{2,3},{3,2},{4,5},{5,4},{6,8},{7,9},{8,6},{9,7},{10,11... | collective-permute-start | bytes 98312 | tf_op jit(solution)/shard_map/ppermute | solution.py:72
  30.2 3.9 %collective-permute-start.16 = (bf16[64,256]{1,0:T(8,128)(2,1)S(1)}, bf16[64,256]{1,0:T(8,128)(2,1)S(1)}, u32[]{:S(2)}, u32[]{:S(2)}) collective-permute-start(bf16[64,256]{1,0:T(8,128)(2,1)S(1)} %get-tuple-element.97), channel_id=1, source_target_pairs={{0,1},{1,0},{2,4},{3,5},{4,2},{5,3},{6,7},{7,6},{8,9},{9,8},{10,12... | collective-permute-start | bytes 98312 | tf_op jit(solution)/shard_map/ppermute | solution.py:72
  31.9 2.2 %collective-permute-start.17 = (bf16[64,256]{1,0:T(8,128)(2,1)S(1)}, bf16[64,256]{1,0:T(8,128)(2,1)S(1)}, u32[]{:S(2)}, u32[]{:S(2)}) collective-permute-start(bf16[64,256]{1,0:T(8,128)(2,1)S(1)} %get-tuple-element.98), channel_id=1, source_target_pairs={{0,2},{1,3},{2,0},{3,1},{4,6},{5,7},{6,4},{7,5},{8,10},{9,11},{10,... | collective-permute-start | bytes 98312 | tf_op jit(solution)/shard_map/ppermute | solution.py:72
  34.3 4.0 %collective-permute-start.18 = (bf16[64,256]{1,0:T(8,128)(2,1)S(1)}, bf16[64,256]{1,0:T(8,128)(2,1)S(1)}, u32[]{:S(2)}, u32[]{:S(2)}) collective-permute-start(bf16[64,256]{1,0:T(8,128)(2,1)S(1)} %get-tuple-element.102), channel_id=1, source_target_pairs={{0,1},{1,0},{2,3},{3,2},{4,5},{5,4},{6,8},{7,9},{8,6},{9,7},{10,11... | collective-permute-start | bytes 98312 | tf_op jit(solution)/shard_map/ppermute | solution.py:72
  36.1 3.9 %collective-permute-start.19 = (bf16[64,256]{1,0:T(8,128)(2,1)S(1)}, bf16[64,256]{1,0:T(8,128)(2,1)S(1)}, u32[]{:S(2)}, u32[]{:S(2)}) collective-permute-start(bf16[64,256]{1,0:T(8,128)(2,1)S(1)} %get-tuple-element.103), channel_id=1, source_target_pairs={{0,1},{1,0},{2,4},{3,5},{4,2},{5,3},{6,7},{7,6},{8,9},{9,8},{10,12... | collective-permute-start | bytes 98312 | tf_op jit(solution)/shard_map/ppermute | solution.py:72
  36.4 3.6 %collective-permute-start.20 = (bf16[64,256]{1,0:T(8,128)(2,1)S(1)}, bf16[64,256]{1,0:T(8,128)(2,1)S(1)}, u32[]{:S(2)}, u32[]{:S(2)}) collective-permute-start(bf16[64,256]{1,0:T(8,128)(2,1)S(1)} %get-tuple-element.104), channel_id=1, source_target_pairs={{0,2},{1,3},{2,0},{3,1},{4,6},{5,7},{6,4},{7,5},{8,10},{9,11},{10,... | collective-permute-start | bytes 98312 | tf_op jit(solution)/shard_map/ppermute | solution.py:72
where the time goes:
time: 73.4 us; the launch traced here: 73.2 us
  blocking collectives  30.8 us (42%)
  starting transfers between devices  17.7 us (24%)
  Pallas kernels  13.8 us (19%)
  waiting for transfers between devices  9.09 us (12%)
  local copies, waits for them, and re-layouts  0.97 us (1%)
  between operations  0.82 us (1%)
    ppermute x21, starting transfers between devices, swap(): lax.ppermute(m, ('wide', 'narrow'), list(f[-1]))  17.7 us
    all_to_all x1, blocking collectives, smooth_by_columns(): lax.all_to_all(wire.reshape(devices, group, own), ('narrow', 'wide'), spl...  15.6 us
    all_to_all x1, blocking collectives, smooth_by_columns(): lax.all_to_all(mixed.reshape(devices, group, own), ('narrow', 'wide'), sp...  15.2 us
    pallas_call x21, Pallas kernels, call(): pl.pallas_call(body, out_shape=outs, in_specs=specs or [VM] * len(args),...  13.8 us
    ppermute x21, waiting for transfers between devices, swap(): lax.ppermute(m, ('wide', 'narrow'), list(f[-1]))  9.09 us
  transfers between devices with their start and end apart: 21, of which 12 were waited for; matrix products, arithmetic and copies ran while one was open for 0% of the time, Pallas kernels for 14%

commit v1 on v0

--- a/solution.py
+++ b/solution.py
@@ -95,6 +95,16 @@
         compiler_params=pltpu.CompilerParams(vmem_limit_bytes=limit * 1024 * 1024),
         cost_estimate=pl.CostEstimate(flops=flops, bytes_accessed=size, transcendentals=0),
     )(*args)
+
+
+def exchange_columns(values):
+    wide, narrow = lax.axis_size("wide"), lax.axis_size("narrow")
+    rows, lanes = values.shape
+    devices = wide * narrow
+    group, parts = rows // devices, lanes // LANES
+    cut = values.reshape(devices, group, parts, LANES).transpose(0, 2, 1, 3).reshape(devices, -1, LANES)
+    moved = lax.all_to_all(cut, ("narrow", "wide"), split_axis=0, concat_axis=0, tiled=True)
+    return moved.reshape(devices, parts, group, LANES).transpose(0, 2, 1, 3).reshape(rows, lanes)
 
 
 def join_halo(got):
@@ -378,13 +388,11 @@
     (order, halo_table), (plane_mix, spread, vert_mix) = tables
     (turned,) = call(turn_body, [shape((columns, own), F32)], [state, order])
     (wire,) = call(functools.partial(wire_body, len(got)), [shape((columns, own), BF)], [turned, halo_table, *got])
-    there = lax.all_to_all(
-        wire.reshape(devices, group, own), ("narrow", "wide"), split_axis=0, concat_axis=0, tiled=True
-    )
+    there = exchange_columns(wire)
     mixed, adjoint = call(
         functools.partial(mix_body, wide, narrow, group),
         [shape((columns, own), BF), shape((own, columns), BF)],
-        [there.reshape(columns, own), plane_mix, spread, vert_mix, state, inverse_halo, *got],
+        [there, plane_mix, spread, vert_mix, state, inverse_halo, *got],
         [
             pltpu.VMEM((tile, wide * group + group, depth), F32),
             pltpu.VMEM((plane_mix.shape[0], group * depth), BF),
@@ -394,13 +402,11 @@
         ],
         out_specs=[VM, ANY],
     )
-    back = lax.all_to_all(
-        mixed.reshape(devices, group, own), ("narrow", "wide"), split_axis=0, concat_axis=0, tiled=True
-    )
+    back = exchange_columns(mixed)
     (smoothed,) = call(
         unwire_body,
         [shape((own, columns), BF)],
-        [back.reshape(columns, own)],
+        [back],
         [pltpu.VMEM((own, columns), BF), pltpu.SemaphoreType.DMA((4,))],
         out_specs=[ANY],
     )

time: 73.4 us -> 73.4 us (level)
  no operation moved by 1% of the time
where the time goes in v1:
time: 73.4 us; the launch traced here: 73.2 us
  blocking collectives  30.8 us (42%)
  starting transfers between devices  17.7 us (24%)
  Pallas kernels  13.8 us (19%)
  waiting for transfers between devices  9.09 us (12%)
  local copies, waits for them, and re-layouts  0.97 us (1%)
  between operations  0.82 us (1%)
    all_to_all x2, blocking collectives, exchange_columns(): lax.all_to_all(cut, ('narrow', 'wide'), split_axis=0, concat_axis=0, tile...  30.8 us
    ppermute x21, starting transfers between devices, swap(): lax.ppermute(m, ('wide', 'narrow'), list(f[-1]))  17.7 us
    pallas_call x21, Pallas kernels, call(): pl.pallas_call(body, out_shape=outs, in_specs=specs or [VM] * len(args),...  13.8 us
    ppermute x21, waiting for transfers between devices, swap(): lax.ppermute(m, ('wide', 'narrow'), list(f[-1]))  9.09 us
  transfers between devices with their start and end apart: 21, of which 12 were waited for; matrix products, arithmetic and copies ran while one was open for 0% of the time, Pallas kernels for 14%

profile of v1, /device:TPU:0, one launch (start us, length us, event | category | flops | bytes accessed | tf_op | source)
XLA Modules:
  0.0 73.2 jit_solution(1784899844616191166)
XLA Ops:
  0.6 0.7 copy-done.5
  1.9 3.0 %collective-permute-start = (bf16[64,256]{1,0:T(8,128)(2,1)S(1)}, bf16[64,256]{1,0:T(8,128)(2,1)S(1)}, u32[]{:S(2)}, u32[]{:S(2)}) collective-permute-start(bf16[64,256]{1,0:T(8,128)(2,1)S(1)} %get-tuple-element.63), channel_id=1, source_target_pairs={{0,1},{1,0},{2,3},{3,2},{4,5},{5,4},{6,8},{7,9},{8,6},{9,7},{10,11... | collective-permute-start | bytes 98312 | tf_op jit(solution)/shard_map/ppermute | solution.py:72
  5.0 1.6 %collective-permute-start.2 = (bf16[64,256]{1,0:T(8,128)(2,1)S(1)}, bf16[64,256]{1,0:T(8,128)(2,1)S(1)}, u32[]{:S(2)}, u32[]{:S(2)}) collective-permute-start(bf16[64,256]{1,0:T(8,128)(2,1)S(1)} %get-tuple-element.65), channel_id=1, source_target_pairs={{0,2},{1,3},{2,0},{3,1},{4,6},{5,7},{6,4},{7,5},{8,10},{9,11},{10,... | collective-permute-start | bytes 98312 | tf_op jit(solution)/shard_map/ppermute | solution.py:72
  6.6 1.6 %shard_map.88 = (bf16[768,256]{1,0:T(8,128)(2,1)S(1)}, bf16[2,768,256]{2,1,0:T(8,128)(2,1)S(1)}, bf16[192,256]{1,0:T(8,128)(2,1)S(1)}, bf16[384,256]{1,0:T(8,128...) custom-call(s32[6,3]{1,0:T(8,128)S(1)} %bitcast.44, bf16[768,1024]{1,0:T(8,128)(2,1)S(1)} %bitcast.27, ...), custom_call_target="tpu_custom_call" | custom-call | bytes 2850888 | tf_op jit(solution)/shard_map/pallas_call | solution.py:89
  8.2 0.6 collective-permute-done.1.rest_1_
  9.4 1.7 %collective-permute-start.4 = (bf16[64,256]{1,0:T(8,128)(2,1)S(1)}, bf16[64,256]{1,0:T(8,128)(2,1)S(1)}, u32[]{:S(2)}, u32[]{:S(2)}) collective-permute-start(bf16[64,256]{1,0:T(8,128)(2,1)S(1)} %get-tuple-element.73), channel_id=1, source_target_pairs={{0,1},{1,0},{2,4},{3,5},{4,2},{5,3},{6,7},{7,6},{8,9},{9,8},{10,12... | collective-permute-start | bytes 98312 | tf_op jit(solution)/shard_map/ppermute | solution.py:72
  11.1 1.1 %shard_map.91 = (f32[768,256]{1,0:T(8,128)S(1)}, f32[768,256]{1,0:T(8,128)S(1)}, f32[192,256]{1,0:T(8,128)S(1)}) custom-call(s32[6,3]{1,0:T(8,128)S(1)} %bitcast.45, f32[768,256]{1,0:T(8,128)S(1)} %get-tuple-element.62.state_ref, bf16[768,256]{1,0:T(8,128)(2,1)S(1)} %get-tuple-element.59.inverse_halo_ref, bf16[6,3,128,128]{3,2,1,0:T(8,128)(2,1)S(1)} %bitcast.32, ...), custom_call_target="tpu_custom_call" | custom-call | bytes 2555976 | tf_op jit(solution)/shard_map/pallas_call | solution.py:89
  12.2 0.8 %collective-permute-done.3.rest_0_ = bf16[64,256]{1,0:T(8,128)(2,1)S(1)} collective-permute-done((bf16[64,256]{1,0:T(8,128)(2,1)S(1)}, bf16[64,256]{1,0:T(8,128)(2,1)S(1)}, u32[]{:S(2)}, u32[]{:S(2)}) %collective-permute-start.3) | collective-permute-done | bytes 32800 | tf_op jit(solution)/shard_map/ppermute | solution.py:72
  13.5 1.7 %collective-permute-start.6 = (bf16[64,256]{1,0:T(8,128)(2,1)S(1)}, bf16[64,256]{1,0:T(8,128)(2,1)S(1)}, u32[]{:S(2)}, u32[]{:S(2)}) collective-permute-start(bf16[64,256]{1,0:T(8,128)(2,1)S(1)} %get-tuple-element.78), channel_id=1, source_target_pairs={{0,1},{1,0},{2,3},{3,2},{4,5},{5,4},{6,8},{7,9},{8,6},{9,7},{10,11... | collective-permute-start | bytes 98312 | tf_op jit(solution)/shard_map/ppermute | solution.py:72
  15.6 0.5 collective-permute-start.8
  16.1 0.7 shard_map.89
  16.8 1.2 %shard_map.93 = (f32[768,256]{1,0:T(8,128)S(1)}, f32[192,256]{1,0:T(8,128)S(1)}) custom-call(f32[768,256]{1,0:T(8,128)S(1)} %get-tuple-element.67.part_ref, bf16[2,768,256]{2,1,0:T(8,128)(2,1)S(1)} %get-tuple-element.68.blocks_halo_ref, f32[768,256]{1,0:T(8,128)S(1)} %get-tuple-element.69.iterate_ref, bf16[768,1024]{1,0:T(8,128)(2,1)S(1)} %bitcast.28, ...), custom_call_target="tpu_custom_call" | custom-call | bytes 4325376 | tf_op jit(solution)/shard_map/pallas_call | solution.py:89
  18.0 1.2 %collective-permute-done.7.rest_1_ = bf16[64,256]{1,0:T(8,128)(2,1)S(1)} collective-permute-done((bf16[64,256]{1,0:T(8,128)(2,1)S(1)}, bf16[64,256]{1,0:T(8,128)(2,1)S(1)}, u32[]{:S(2)}, u32[]{:S(2)}) %collective-permute-start.7) | collective-permute-done | bytes 32800 | tf_op jit(solution)/shard_map/ppermute | solution.py:72
  19.4 0.4 collective-permute-start.10
  19.8 1.7 %collective-permute-start.11 = (bf16[64,256]{1,0:T(8,128)(2,1)S(1)}, bf16[64,256]{1,0:T(8,128)(2,1)S(1)}, u32[]{:S(2)}, u32[]{:S(2)}) collective-permute-start(bf16[64,256]{1,0:T(8,128)(2,1)S(1)} %get-tuple-element.87), channel_id=1, source_target_pairs={{0,1},{1,0},{2,4},{3,5},{4,2},{5,3},{6,7},{7,6},{8,9},{9,8},{10,12... | collective-permute-start | bytes 98312 | tf_op jit(solution)/shard_map/ppermute | solution.py:72
  21.5 1.1 %shard_map.95 = (f32[768,256]{1,0:T(8,128)S(1)}, f32[768,256]{1,0:T(8,128)S(1)}, f32[192,256]{1,0:T(8,128)S(1)}) custom-call(s32[6,3]{1,0:T(8,128)S(1)} %bitcast.46, f32[768,256]{1,0:T(8,128)S(1)} %get-tuple-element.75.state_ref, bf16[768,256]{1,0:T(8,128)(2,1)S(1)} %get-tuple-element.59.inverse_halo_ref, bf16[6,3,128,128]{3,2,1,0:T(8,128)(2,1)S(1)} %bitcast.33, ...), custom_call_target="tpu_custom_call" | custom-call | bytes 2555976 | tf_op jit(solution)/shard_map/pallas_call | solution.py:89
  22.6 0.8 %collective-permute-done.10.rest_1_ = bf16[64,256]{1,0:T(8,128)(2,1)S(1)} collective-permute-done((bf16[64,256]{1,0:T(8,128)(2,1)S(1)}, bf16[64,256]{1,0:T(8,128)(2,1)S(1)}, u32[]{:S(2)}, u32[]{:S(2)}) %collective-permute-start.10) | collective-permute-done | bytes 32800 | tf_op jit(solution)/shard_map/ppermute | solution.py:72
  23.9 1.7 %collective-permute-start.12 = (bf16[64,256]{1,0:T(8,128)(2,1)S(1)}, bf16[64,256]{1,0:T(8,128)(2,1)S(1)}, u32[]{:S(2)}, u32[]{:S(2)}) collective-permute-start(bf16[64,256]{1,0:T(8,128)(2,1)S(1)} %get-tuple-element.90), channel_id=1, source_target_pairs={{0,1},{1,0},{2,3},{3,2},{4,5},{5,4},{6,8},{7,9},{8,6},{9,7},{10,11... | collective-permute-start | bytes 98312 | tf_op jit(solution)/shard_map/ppermute | solution.py:72
  26.0 0.5 shard_map.86
  26.5 1.2 %shard_map.97 = (f32[768,256]{1,0:T(8,128)S(1)}, f32[192,256]{1,0:T(8,128)S(1)}) custom-call(f32[768,256]{1,0:T(8,128)S(1)} %get-tuple-element.82.part_ref, bf16[2,768,256]{2,1,0:T(8,128)(2,1)S(1)} %get-tuple-element.68.blocks_halo_ref, f32[768,256]{1,0:T(8,128)S(1)} %get-tuple-element.83.iterate_ref, bf16[768,1024]{1,0:T(8,128)(2,1)S(1)} %bitcast.29, ...), custom_call_target="tpu_custom_call" | custom-call | bytes 4325376 | tf_op jit(solution)/shard_map/pallas_call | solution.py:89
  27.9 1.7 %collective-permute-done.13.rest_1_ = bf16[64,256]{1,0:T(8,128)(2,1)S(1)} collective-permute-done((bf16[64,256]{1,0:T(8,128)(2,1)S(1)}, bf16[64,256]{1,0:T(8,128)(2,1)S(1)}, u32[]{:S(2)}, u32[]{:S(2)}) %collective-permute-start.13) | collective-permute-done | bytes 32800 | tf_op jit(solution)/shard_map/ppermute | solution.py:72
  30.2 1.7 %collective-permute-start.16 = (bf16[64,256]{1,0:T(8,128)(2,1)S(1)}, bf16[64,256]{1,0:T(8,128)(2,1)S(1)}, u32[]{:S(2)}, u32[]{:S(2)}) collective-permute-start(bf16[64,256]{1,0:T(8,128)(2,1)S(1)} %get-tuple-element.97), channel_id=1, source_target_pairs={{0,1},{1,0},{2,4},{3,5},{4,2},{5,3},{6,7},{7,6},{8,9},{9,8},{10,12... | collective-permute-start | bytes 98312 | tf_op jit(solution)/shard_map/ppermute | solution.py:72
  31.9 1.1 %shard_map.99 = (f32[768,256]{1,0:T(8,128)S(1)}, f32[768,256]{1,0:T(8,128)S(1)}, f32[192,256]{1,0:T(8,128)S(1)}) custom-call(s32[6,3]{1,0:T(8,128)S(1)} %bitcast.47, f32[768,256]{1,0:T(8,128)S(1)} %get-tuple-element.88.state_ref, bf16[768,256]{1,0:T(8,128)(2,1)S(1)} %get-tuple-element.59.inverse_halo_ref, bf16[6,3,128,128]{3,2,1,0:T(8,128)(2,1)S(1)} %bitcast.34, ...), custom_call_target="tpu_custom_call" | custom-call | bytes 2555976 | tf_op jit(solution)/shard_map/pallas_call | solution.py:89
  33.0 0.8 %collective-permute-done.15.rest_0_ = bf16[64,256]{1,0:T(8,128)(2,1)S(1)} collective-permute-done((bf16[64,256]{1,0:T(8,128)(2,1)S(1)}, bf16[64,256]{1,0:T(8,128)(2,1)S(1)}, u32[]{:S(2)}, u32[]{:S(2)}) %collective-permute-start.15) | collective-permute-done | bytes 32800 | tf_op jit(solution)/shard_map/ppermute | solution.py:72
  34.3 1.7 %collective-permute-start.18 = (bf16[64,256]{1,0:T(8,128)(2,1)S(1)}, bf16[64,256]{1,0:T(8,128)(2,1)S(1)}, u32[]{:S(2)}, u32[]{:S(2)}) collective-permute-start(bf16[64,256]{1,0:T(8,128)(2,1)S(1)} %get-tuple-element.102), channel_id=1, source_target_pairs={{0,1},{1,0},{2,3},{3,2},{4,5},{5,4},{6,8},{7,9},{8,6},{9,7},{10,11... | collective-permute-start | bytes 98312 | tf_op jit(solution)/shard_map/ppermute | solution.py:72
  36.4 0.8 %shard_map.101.state_ref = f32[768,256]{1,0:T(8,128)S(1)} custom-call(f32[768,256]{1,0:T(8,128)S(1)} %get-tuple-element.93.part_ref, bf16[2,768,256]{2,1,0:T(8,128)(2,1)S(1)} %get-tuple-element.68.blocks_halo_ref, f32[768,256]{1,0:T(8,128)S(1)} %get-tuple-element.94.iterate_ref, bf16[768,1024]{1,0:T(8,128)(2,1)S(1)} %bitcast.30, ...), custom_call_target="tpu_custom_call" | custom-call | bytes 4325376 | tf_op jit(solution)/shard_map/pallas_call | solution.py:89
  37.2 0.8 %shard_map.102.turned_ref = f32[256,768]{1,0:T(8,128)S(1)} custom-call(f32[768,256]{1,0:T(8,128)S(1)} %shard_map.101.state_ref, bf16[768,768]{1,0:T(8,128)(2,1)S(1)} %get-tuple-element.99.order_ref), custom_call_target="tpu_custom_call" | custom-call | bytes 1966080 | tf_op jit(solution)/shard_map/pallas_call | solution.py:89
  38.3 1.7 %collective-permute-done.19.rest_1_ = bf16[64,256]{1,0:T(8,128)(2,1)S(1)} collective-permute-done((bf16[64,256]{1,0:T(8,128)(2,1)S(1)}, bf16[64,256]{1,0:T(8,128)(2,1)S(1)}, u32[]{:S(2)}, u32[]{:S(2)}) %collective-permute-start.19) | collective-permute-done | bytes 32800 | tf_op jit(solution)/shard_map/ppermute | solution.py:72
  40.3 15.6 %all_to_all.10 = bf16[32,48,128]{2,1,0:T(8,128)(2,1)S(1)} all-to-all(bf16[32,48,128]{2,1,0:T(8,128)(2,1)S(1)} %bitcast.41), channel_id=1, replica_groups=mesh['wide'=16,'narrow'=2] {'narrow','wide'}, dimensions={0} | all-to-all | bytes 786432 | tf_op jit(solution)/shard_map/all_to_all | solution.py:106
  55.8 1.0 %shard_map.105 = (bf16[256,768]{1,0:T(8,128)(2,1)S(1)}, bf16[768,256]{1,0:T(8,128)(2,1)}) custom-call(bf16[256,768]{1,0:T(8,128)(2,1)S(1)} %bitcast.42, bf16[192,192]{1,0:T(8,128)(2,1)S(1)} %get-tuple-element.105.plane_ref, bf16[256,256]{1,0:T(8,128)(2,1)S(1)} %get-tuple-element.106.spread_ref, bf16[256,256]{1,0:T(8,128)(2,1)S(1)} %get-tuple-element.107.vert_ref, ...), custom_call_target="tpu_custom_call" | custom-call | bytes 2007040 | tf_op jit(solution)/shard_map/pallas_call | solution.py:89
  56.9 15.2 %all_to_all.11 = bf16[32,48,128]{2,1,0:T(8,128)(2,1)S(1)} all-to-all(bf16[32,48,128]{2,1,0:T(8,128)(2,1)S(1)} %bitcast.43), channel_id=1, replica_groups=mesh['wide'=16,'narrow'=2] {'narrow','wide'}, dimensions={0} | all-to-all | bytes 786432 | tf_op jit(solution)/shard_map/all_to_all | solution.py:106
  72.1 1.1 %shard_map.106 = bf16[768,256]{1,0:T(8,128)(2,1)} custom-call(bf16[256,768]{1,0:T(8,128)(2,1)S(1)} %bitcast.40), custom_call_target="tpu_custom_call" | custom-call | bytes 393216 | tf_op jit(solution)/shard_map/pallas_call | solution.py:89
  (48 shorter events, 5.6 us)
Async XLA Ops:
  0.6 1.0 %copy-start.2 = (bf16[1,1,768,256]{3,2,1,0:T(8,128)(2,1)S(1)}, bf16[1,1,768,256]{3,2,1,0:T(8,128)(2,1)}, u32[]{:S(2)}) copy-start(bf16[1,1,768,256]{3,2,1,0:T(8,128)(2,1)} %param.7) | copy-start | bytes 1179652
  0.6 0.7 %copy-start.5 = (s32[1,1,4,64]{3,2,1,0:T(4,128)S(1)}, s32[1,1,4,64]{3,2,1,0:T(4,128)}, u32[]{:S(2)}) copy-start(s32[1,1,4,64]{3,2,1,0:T(4,128)} %param.11) | copy-start | bytes 3076
  1.6 4.9 %copy-start.6 = (s32[1,1,6,3]{2,1,3,0:T(1,128)S(1)}, s32[1,1,6,3]{2,1,3,0:T(1,128)}, u32[]{:S(2)}) copy-start(s32[1,1,6,3]{2,1,3,0:T(1,128)} %param.10) | copy-start | bytes 220
  1.6 5.0 %copy-start = (bf16[1,1,768,1024]{3,2,1,0:T(8,128)(2,1)S(1)}, bf16[1,1,768,1024]{3,2,1,0:T(8,128)(2,1)}, u32[]{:S(2)}) copy-start(bf16[1,1,768,1024]{3,2,1,0:T(8,128)(2,1)} %param.8) | copy-start | bytes 4718596
  1.6 5.0 %copy-start.1 = (bf16[1,1,6,3,128,128]{5,4,3,2,1,0:T(8,128)(2,1)S(1)}, bf16[1,1,6,3,128,128]{5,4,3,2,1,0:T(8,128)(2,1)}, u32[]{:S(2)}) copy-start(bf16[1,1,6,3,128,128]{5,4,3,2,1,0:T(8,128)(2,1)} %param.9) | copy-start | bytes 1769476
  1.9 6.3 %collective-permute-start = (bf16[64,256]{1,0:T(8,128)(2,1)S(1)}, bf16[64,256]{1,0:T(8,128)(2,1)S(1)}, u32[]{:S(2)}, u32[]{:S(2)}) collective-permute-start(bf16[64,256]{1,0:T(8,128)(2,1)S(1)} %get-tuple-element.63), channel_id=1, source_target_pairs={{0,1},{1,0},{2,3},{3,2},{4,5},{5,4},{6,8},{7,9},{8,6},{9,7},{10,11... | collective-permute-start | bytes 98312 | tf_op jit(solution)/shard_map/ppermute | solution.py:72
  4.9 3.9 %collective-permute-start.1 = (bf16[64,256]{1,0:T(8,128)(2,1)S(1)}, bf16[64,256]{1,0:T(8,128)(2,1)S(1)}, u32[]{:S(2)}, u32[]{:S(2)}) collective-permute-start(bf16[64,256]{1,0:T(8,128)(2,1)S(1)} %get-tuple-element.64), channel_id=1, source_target_pairs={{0,1},{1,0},{2,4},{3,5},{4,2},{5,3},{6,7},{7,6},{8,9},{9,8},{10,12... | collective-permute-start | bytes 98312 | tf_op jit(solution)/shard_map/ppermute | solution.py:72
  5.0 3.8 %collective-permute-start.2 = (bf16[64,256]{1,0:T(8,128)(2,1)S(1)}, bf16[64,256]{1,0:T(8,128)(2,1)S(1)}, u32[]{:S(2)}, u32[]{:S(2)}) collective-permute-start(bf16[64,256]{1,0:T(8,128)(2,1)S(1)} %get-tuple-element.65), channel_id=1, source_target_pairs={{0,2},{1,3},{2,0},{3,1},{4,6},{5,7},{6,4},{7,5},{8,10},{9,11},{10,... | collective-permute-start | bytes 98312 | tf_op jit(solution)/shard_map/ppermute | solution.py:72
  9.0 4.0 %collective-permute-start.3 = (bf16[64,256]{1,0:T(8,128)(2,1)S(1)}, bf16[64,256]{1,0:T(8,128)(2,1)S(1)}, u32[]{:S(2)}, u32[]{:S(2)}) collective-permute-start(bf16[64,256]{1,0:T(8,128)(2,1)S(1)} %get-tuple-element.72), channel_id=1, source_target_pairs={{0,1},{1,0},{2,3},{3,2},{4,5},{5,4},{6,8},{7,9},{8,6},{9,7},{10,11... | collective-permute-start | bytes 98312 | tf_op jit(solution)/shard_map/ppermute | solution.py:72
  9.4 3.9 %collective-permute-start.4 = (bf16[64,256]{1,0:T(8,128)(2,1)S(1)}, bf16[64,256]{1,0:T(8,128)(2,1)S(1)}, u32[]{:S(2)}, u32[]{:S(2)}) collective-permute-start(bf16[64,256]{1,0:T(8,128)(2,1)S(1)} %get-tuple-element.73), channel_id=1, source_target_pairs={{0,1},{1,0},{2,4},{3,5},{4,2},{5,3},{6,7},{7,6},{8,9},{9,8},{10,12... | collective-permute-start | bytes 98312 | tf_op jit(solution)/shard_map/ppermute | solution.py:72
  11.1 2.2 %collective-permute-start.5 = (bf16[64,256]{1,0:T(8,128)(2,1)S(1)}, bf16[64,256]{1,0:T(8,128)(2,1)S(1)}, u32[]{:S(2)}, u32[]{:S(2)}) collective-permute-start(bf16[64,256]{1,0:T(8,128)(2,1)S(1)} %get-tuple-element.74), channel_id=1, source_target_pairs={{0,2},{1,3},{2,0},{3,1},{4,6},{5,7},{6,4},{7,5},{8,10},{9,11},{10,... | collective-permute-start | bytes 98312 | tf_op jit(solution)/shard_map/ppermute | solution.py:72
  13.5 4.4 %collective-permute-start.6 = (bf16[64,256]{1,0:T(8,128)(2,1)S(1)}, bf16[64,256]{1,0:T(8,128)(2,1)S(1)}, u32[]{:S(2)}, u32[]{:S(2)}) collective-permute-start(bf16[64,256]{1,0:T(8,128)(2,1)S(1)} %get-tuple-element.78), channel_id=1, source_target_pairs={{0,1},{1,0},{2,3},{3,2},{4,5},{5,4},{6,8},{7,9},{8,6},{9,7},{10,11... | collective-permute-start | bytes 98312 | tf_op jit(solution)/shard_map/ppermute | solution.py:72
  15.3 3.9 %collective-permute-start.7 = (bf16[64,256]{1,0:T(8,128)(2,1)S(1)}, bf16[64,256]{1,0:T(8,128)(2,1)S(1)}, u32[]{:S(2)}, u32[]{:S(2)}) collective-permute-start(bf16[64,256]{1,0:T(8,128)(2,1)S(1)} %get-tuple-element.79), channel_id=1, source_target_pairs={{0,1},{1,0},{2,4},{3,5},{4,2},{5,3},{6,7},{7,6},{8,9},{9,8},{10,12... | collective-permute-start | bytes 98312 | tf_op jit(solution)/shard_map/ppermute | solution.py:72
  15.6 3.6 %collective-permute-start.8 = (bf16[64,256]{1,0:T(8,128)(2,1)S(1)}, bf16[64,256]{1,0:T(8,128)(2,1)S(1)}, u32[]{:S(2)}, u32[]{:S(2)}) collective-permute-start(bf16[64,256]{1,0:T(8,128)(2,1)S(1)} %get-tuple-element.80), channel_id=1, source_target_pairs={{0,2},{1,3},{2,0},{3,1},{4,6},{5,7},{6,4},{7,5},{8,10},{9,11},{10,... | collective-permute-start | bytes 98312 | tf_op jit(solution)/shard_map/ppermute | solution.py:72
  19.4 6.7 %copy-start.3 = (bf16[192,192]{1,0:T(8,128)(2,1)S(1)}, bf16[192,192]{1,0:T(8,128)(2,1)}, u32[]{:S(2)}) copy-start(bf16[192,192]{1,0:T(8,128)(2,1)} %cov_plane_ref.1) | copy-start | bytes 221188
  19.4 6.7 %copy-start.4 = (bf16[128,128]{1,0:T(8,128)(2,1)S(1)}, bf16[128,128]{1,0:T(8,128)(2,1)}, u32[]{:S(2)}) copy-start(bf16[128,128]{1,0:T(8,128)(2,1)} %cov_vert_ref.1) | copy-start | bytes 98308
  19.4 4.0 %collective-permute-start.10 = (bf16[64,256]{1,0:T(8,128)(2,1)S(1)}, bf16[64,256]{1,0:T(8,128)(2,1)S(1)}, u32[]{:S(2)}, u32[]{:S(2)}) collective-permute-start(bf16[64,256]{1,0:T(8,128)(2,1)S(1)} %get-tuple-element.86), channel_id=1, source_target_pairs={{0,1},{1,0},{2,3},{3,2},{4,5},{5,4},{6,8},{7,9},{8,6},{9,7},{10,11... | collective-permute-start | bytes 98312 | tf_op jit(solution)/shard_map/ppermute | solution.py:72
  19.8 3.9 %collective-permute-start.11 = (bf16[64,256]{1,0:T(8,128)(2,1)S(1)}, bf16[64,256]{1,0:T(8,128)(2,1)S(1)}, u32[]{:S(2)}, u32[]{:S(2)}) collective-permute-start(bf16[64,256]{1,0:T(8,128)(2,1)S(1)} %get-tuple-element.87), channel_id=1, source_target_pairs={{0,1},{1,0},{2,4},{3,5},{4,2},{5,3},{6,7},{7,6},{8,9},{9,8},{10,12... | collective-permute-start | bytes 98312 | tf_op jit(solution)/shard_map/ppermute | solution.py:72
  21.5 2.2 %collective-permute-start.9 = (bf16[64,256]{1,0:T(8,128)(2,1)S(1)}, bf16[64,256]{1,0:T(8,128)(2,1)S(1)}, u32[]{:S(2)}, u32[]{:S(2)}) collective-permute-start(bf16[64,256]{1,0:T(8,128)(2,1)S(1)} %get-tuple-element.85), channel_id=1, source_target_pairs={{0,2},{1,3},{2,0},{3,1},{4,6},{5,7},{6,4},{7,5},{8,10},{9,11},{10,... | collective-permute-start | bytes 98312 | tf_op jit(solution)/shard_map/ppermute | solution.py:72
  23.9 4.0 %collective-permute-start.12 = (bf16[64,256]{1,0:T(8,128)(2,1)S(1)}, bf16[64,256]{1,0:T(8,128)(2,1)S(1)}, u32[]{:S(2)}, u32[]{:S(2)}) collective-permute-start(bf16[64,256]{1,0:T(8,128)(2,1)S(1)} %get-tuple-element.90), channel_id=1, source_target_pairs={{0,1},{1,0},{2,3},{3,2},{4,5},{5,4},{6,8},{7,9},{8,6},{9,7},{10,11... | collective-permute-start | bytes 98312 | tf_op jit(solution)/shard_map/ppermute | solution.py:72
  25.7 3.9 %collective-permute-start.13 = (bf16[64,256]{1,0:T(8,128)(2,1)S(1)}, bf16[64,256]{1,0:T(8,128)(2,1)S(1)}, u32[]{:S(2)}, u32[]{:S(2)}) collective-permute-start(bf16[64,256]{1,0:T(8,128)(2,1)S(1)} %get-tuple-element.91), channel_id=1, source_target_pairs={{0,1},{1,0},{2,4},{3,5},{4,2},{5,3},{6,7},{7,6},{8,9},{9,8},{10,12... | collective-permute-start | bytes 98312 | tf_op jit(solution)/shard_map/ppermute | solution.py:72
  26.0 3.6 %collective-permute-start.14 = (bf16[64,256]{1,0:T(8,128)(2,1)S(1)}, bf16[64,256]{1,0:T(8,128)(2,1)S(1)}, u32[]{:S(2)}, u32[]{:S(2)}) collective-permute-start(bf16[64,256]{1,0:T(8,128)(2,1)S(1)} %get-tuple-element.92), channel_id=1, source_target_pairs={{0,2},{1,3},{2,0},{3,1},{4,6},{5,7},{6,4},{7,5},{8,10},{9,11},{10,... | collective-permute-start | bytes 98312 | tf_op jit(solution)/shard_map/ppermute | solution.py:72
  29.8 4.0 %collective-permute-start.15 = (bf16[64,256]{1,0:T(8,128)(2,1)S(1)}, bf16[64,256]{1,0:T(8,128)(2,1)S(1)}, u32[]{:S(2)}, u32[]{:S(2)}) collective-permute-start(bf16[64,256]{1,0:T(8,128)(2,1)S(1)} %get-tuple-element.96), channel_id=1, source_target_pairs={{0,1},{1,0},{2,3},{3,2},{4,5},{5,4},{6,8},{7,9},{8,6},{9,7},{10,11... | collective-permute-start | bytes 98312 | tf_op jit(solution)/shard_map/ppermute | solution.py:72
  30.2 3.9 %collective-permute-start.16 = (bf16[64,256]{1,0:T(8,128)(2,1)S(1)}, bf16[64,256]{1,0:T(8,128)(2,1)S(1)}, u32[]{:S(2)}, u32[]{:S(2)}) collective-permute-start(bf16[64,256]{1,0:T(8,128)(2,1)S(1)} %get-tuple-element.97), channel_id=1, source_target_pairs={{0,1},{1,0},{2,4},{3,5},{4,2},{5,3},{6,7},{7,6},{8,9},{9,8},{10,12... | collective-permute-start | bytes 98312 | tf_op jit(solution)/shard_map/ppermute | solution.py:72
  31.9 2.2 %collective-permute-start.17 = (bf16[64,256]{1,0:T(8,128)(2,1)S(1)}, bf16[64,256]{1,0:T(8,128)(2,1)S(1)}, u32[]{:S(2)}, u32[]{:S(2)}) collective-permute-start(bf16[64,256]{1,0:T(8,128)(2,1)S(1)} %get-tuple-element.98), channel_id=1, source_target_pairs={{0,2},{1,3},{2,0},{3,1},{4,6},{5,7},{6,4},{7,5},{8,10},{9,11},{10,... | collective-permute-start | bytes 98312 | tf_op jit(solution)/shard_map/ppermute | solution.py:72
  34.3 4.0 %collective-permute-start.18 = (bf16[64,256]{1,0:T(8,128)(2,1)S(1)}, bf16[64,256]{1,0:T(8,128)(2,1)S(1)}, u32[]{:S(2)}, u32[]{:S(2)}) collective-permute-start(bf16[64,256]{1,0:T(8,128)(2,1)S(1)} %get-tuple-element.102), channel_id=1, source_target_pairs={{0,1},{1,0},{2,3},{3,2},{4,5},{5,4},{6,8},{7,9},{8,6},{9,7},{10,11... | collective-permute-start | bytes 98312 | tf_op jit(solution)/shard_map/ppermute | solution.py:72
  36.1 3.9 %collective-permute-start.19 = (bf16[64,256]{1,0:T(8,128)(2,1)S(1)}, bf16[64,256]{1,0:T(8,128)(2,1)S(1)}, u32[]{:S(2)}, u32[]{:S(2)}) collective-permute-start(bf16[64,256]{1,0:T(8,128)(2,1)S(1)} %get-tuple-element.103), channel_id=1, source_target_pairs={{0,1},{1,0},{2,4},{3,5},{4,2},{5,3},{6,7},{7,6},{8,9},{9,8},{10,12... | collective-permute-start | bytes 98312 | tf_op jit(solution)/shard_map/ppermute | solution.py:72
  36.4 3.6 %collective-permute-start.20 = (bf16[64,256]{1,0:T(8,128)(2,1)S(1)}, bf16[64,256]{1,0:T(8,128)(2,1)S(1)}, u32[]{:S(2)}, u32[]{:S(2)}) collective-permute-start(bf16[64,256]{1,0:T(8,128)(2,1)S(1)} %get-tuple-element.104), channel_id=1, source_target_pairs={{0,2},{1,3},{2,0},{3,1},{4,6},{5,7},{6,4},{7,5},{8,10},{9,11},{10,... | collective-permute-start | bytes 98312 | tf_op jit(solution)/shard_map/ppermute | solution.py:72

commit v2 on v0

--- a/solution.py
+++ b/solution.py
@@ -170,14 +170,13 @@
 
 def sent_update_body(count, base_ref, sent_ref, *rest):
     got, messages = rest[:count], rest[count:]
-    halo = jnp.concatenate([piece[...] for piece in got], axis=0)
-    send(messages, base_ref[...] + mm(sent_ref[:, :halo.shape[0]], halo))
+    send(messages, base_ref[...] + mm(sent_ref[...], join_halo(got)))
 
 
 def sent_residual_body(count, turn, base_ref, sent_ref, *rest):
     got, messages = rest[:count], rest[count:]
-    halo = jnp.concatenate([piece[...] for piece in got[turn:] + got[:turn]], axis=0)
-    part = mm(sent_ref[:, :halo.shape[0]], halo)
+    halo = join_halo(got[turn:] + got[:turn])
+    part = mm(sent_ref[...], halo)
     sent = base_ref.shape[0]
     send(messages, base_ref[...] - (part[:sent] + part[sent:]))
 
@@ -296,19 +295,29 @@
     share = LANES // ZL
     depth = narrow * ZL
     block = wide * group
-    for g in range(tile // share):
-        lanes = slice(g * LANES, (g + 1) * LANES)
-        joined = jnp.concatenate([in_ref[n * block:(n + 1) * block, lanes] for n in range(narrow)], axis=1)
+    pairs = tile // share
+    halves = [range(0, pairs // 2), range(pairs // 2, pairs)]
+    for half in halves:
+        joined = jnp.concatenate(
+            [
+                jnp.concatenate(
+                    [in_ref[n * block:(n + 1) * block, g * LANES:(g + 1) * LANES] for n in range(narrow)], axis=1
+                )
+                for g in half
+            ],
+            axis=0,
+        )
         spread = mm(joined, spread_ref[...])
-        for e in range(share):
-            cells_ref[g * share + e, :block, :] = spread[:, e * depth:(e + 1) * depth]
+        for i, g in enumerate(half):
+            for e in range(share):
+                cells_ref[g * share + e, :block, :] = spread[i * block:(i + 1) * block, e * depth:(e + 1) * depth]
     for r in range(group):
         for c in range(tile):
             flat_ref[c * wide:(c + 1) * wide, r * depth:(r + 1) * depth] = cells_ref[
                 c, pl.ds(r, wide, stride=group), :
             ].astype(BF)
     planar = mm(plane_ref[...], flat_ref[...]).astype(BF)
-    for g in range(tile // share):
+    for half in halves:
         stacked = jnp.concatenate(
             [
                 jnp.concatenate(
@@ -318,17 +327,20 @@
                     ],
                     axis=1,
                 )
+                for g in half
                 for r in range(group)
             ],
             axis=0,
         )
         mixed = mm(stacked, vert_ref[...])
-        for r in range(group):
-            for n in range(narrow):
-                wire_ref[g, pl.ds(n * block + r, wide, stride=group), :] = mixed[
-                    r * wide:(r + 1) * wide, n * LANES:(n + 1) * LANES
-                ]
-        out_ref[:, g * LANES:(g + 1) * LANES] = wire_ref[g, :narrow * block, :].astype(BF)
+        for i, g in enumerate(half):
+            for r in range(group):
+                rows = slice(i * block + r * wide, i * block + (r + 1) * wide)
+                for n in range(narrow):
+                    wire_ref[g, pl.ds(n * block + r, wide, stride=group), :] = mixed[
+                        rows, n * LANES:(n + 1) * LANES
+                    ]
+            out_ref[:, g * LANES:(g + 1) * LANES] = wire_ref[g, :narrow * block, :].astype(BF)
     keep.wait()
 
 

time: 73.4 us -> 73.4 us (level)
  no operation moved by 1% of the time
where the time goes in v2:
time: 73.4 us; the launch traced here: 73.2 us
  blocking collectives  30.8 us (42%)
  starting transfers between devices  17.7 us (24%)
  Pallas kernels  13.8 us (19%)
  waiting for transfers between devices  9.09 us (12%)
  local copies, waits for them, and re-layouts  0.97 us (1%)
  between operations  0.83 us (1%)
    ppermute x21, starting transfers between devices, swap(): lax.ppermute(m, ('wide', 'narrow'), list(f[-1]))  17.7 us
    all_to_all x1, blocking collectives, smooth_by_columns(): lax.all_to_all(wire.reshape(devices, group, own), ('narrow', 'wide'), spl...  15.5 us
    all_to_all x1, blocking collectives, smooth_by_columns(): lax.all_to_all(mixed.reshape(devices, group, own), ('narrow', 'wide'), sp...  15.2 us
    pallas_call x21, Pallas kernels, call(): pl.pallas_call(body, out_shape=outs, in_specs=specs or [VM] * len(args),...  13.8 us
    ppermute x21, waiting for transfers between devices, swap(): lax.ppermute(m, ('wide', 'narrow'), list(f[-1]))  9.09 us
  transfers between devices with their start and end apart: 21, of which 12 were waited for; matrix products, arithmetic and copies ran while one was open for 0% of the time, Pallas kernels for 14%

profile of v2, /device:TPU:0, one launch (start us, length us, event | category | flops | bytes accessed | tf_op | source)
XLA Modules:
  0.0 73.2 jit_solution(11983871826549544605)
XLA Ops:
  0.6 0.7 copy-done.5
  1.9 3.0 %collective-permute-start = (bf16[64,256]{1,0:T(8,128)(2,1)S(1)}, bf16[64,256]{1,0:T(8,128)(2,1)S(1)}, u32[]{:S(2)}, u32[]{:S(2)}) collective-permute-start(bf16[64,256]{1,0:T(8,128)(2,1)S(1)} %get-tuple-element.63), channel_id=1, source_target_pairs={{0,1},{1,0},{2,3},{3,2},{4,5},{5,4},{6,8},{7,9},{8,6},{9,7},{10,11... | collective-permute-start | bytes 98312 | tf_op jit(solution)/shard_map/ppermute | solution.py:72
  5.0 1.6 %collective-permute-start.2 = (bf16[64,256]{1,0:T(8,128)(2,1)S(1)}, bf16[64,256]{1,0:T(8,128)(2,1)S(1)}, u32[]{:S(2)}, u32[]{:S(2)}) collective-permute-start(bf16[64,256]{1,0:T(8,128)(2,1)S(1)} %get-tuple-element.65), channel_id=1, source_target_pairs={{0,2},{1,3},{2,0},{3,1},{4,6},{5,7},{6,4},{7,5},{8,10},{9,11},{10,... | collective-permute-start | bytes 98312 | tf_op jit(solution)/shard_map/ppermute | solution.py:72
  6.6 1.6 %shard_map.88 = (bf16[768,256]{1,0:T(8,128)(2,1)S(1)}, bf16[2,768,256]{2,1,0:T(8,128)(2,1)S(1)}, bf16[192,256]{1,0:T(8,128)(2,1)S(1)}, bf16[384,256]{1,0:T(8,128...) custom-call(s32[6,3]{1,0:T(8,128)S(1)} %bitcast.28, bf16[768,1024]{1,0:T(8,128)(2,1)S(1)} %bitcast.11, ...), custom_call_target="tpu_custom_call" | custom-call | bytes 2850888 | tf_op jit(solution)/shard_map/pallas_call | solution.py:89
  8.2 0.6 collective-permute-done.1.rest_1_
  9.4 1.7 %collective-permute-start.4 = (bf16[64,256]{1,0:T(8,128)(2,1)S(1)}, bf16[64,256]{1,0:T(8,128)(2,1)S(1)}, u32[]{:S(2)}, u32[]{:S(2)}) collective-permute-start(bf16[64,256]{1,0:T(8,128)(2,1)S(1)} %get-tuple-element.73), channel_id=1, source_target_pairs={{0,1},{1,0},{2,4},{3,5},{4,2},{5,3},{6,7},{7,6},{8,9},{9,8},{10,12... | collective-permute-start | bytes 98312 | tf_op jit(solution)/shard_map/ppermute | solution.py:72
  11.1 1.1 %shard_map.91 = (f32[768,256]{1,0:T(8,128)S(1)}, f32[768,256]{1,0:T(8,128)S(1)}, f32[192,256]{1,0:T(8,128)S(1)}) custom-call(s32[6,3]{1,0:T(8,128)S(1)} %bitcast.29, f32[768,256]{1,0:T(8,128)S(1)} %get-tuple-element.62.state_ref, bf16[768,256]{1,0:T(8,128)(2,1)S(1)} %get-tuple-element.59.inverse_halo_ref, bf16[6,3,128,128]{3,2,1,0:T(8,128)(2,1)S(1)} %bitcast.16, ...), custom_call_target="tpu_custom_call" | custom-call | bytes 2555976 | tf_op jit(solution)/shard_map/pallas_call | solution.py:89
  12.2 0.8 %collective-permute-done.3.rest_0_ = bf16[64,256]{1,0:T(8,128)(2,1)S(1)} collective-permute-done((bf16[64,256]{1,0:T(8,128)(2,1)S(1)}, bf16[64,256]{1,0:T(8,128)(2,1)S(1)}, u32[]{:S(2)}, u32[]{:S(2)}) %collective-permute-start.3) | collective-permute-done | bytes 32800 | tf_op jit(solution)/shard_map/ppermute | solution.py:72
  13.5 1.7 %collective-permute-start.6 = (bf16[64,256]{1,0:T(8,128)(2,1)S(1)}, bf16[64,256]{1,0:T(8,128)(2,1)S(1)}, u32[]{:S(2)}, u32[]{:S(2)}) collective-permute-start(bf16[64,256]{1,0:T(8,128)(2,1)S(1)} %get-tuple-element.78), channel_id=1, source_target_pairs={{0,1},{1,0},{2,3},{3,2},{4,5},{5,4},{6,8},{7,9},{8,6},{9,7},{10,11... | collective-permute-start | bytes 98312 | tf_op jit(solution)/shard_map/ppermute | solution.py:72
  15.6 0.5 collective-permute-start.8
  16.1 0.7 shard_map.89
  16.8 1.2 %shard_map.93 = (f32[768,256]{1,0:T(8,128)S(1)}, f32[192,256]{1,0:T(8,128)S(1)}) custom-call(f32[768,256]{1,0:T(8,128)S(1)} %get-tuple-element.67.part_ref, bf16[2,768,256]{2,1,0:T(8,128)(2,1)S(1)} %get-tuple-element.68.blocks_halo_ref, f32[768,256]{1,0:T(8,128)S(1)} %get-tuple-element.69.iterate_ref, bf16[768,1024]{1,0:T(8,128)(2,1)S(1)} %bitcast.12, ...), custom_call_target="tpu_custom_call" | custom-call | bytes 4325376 | tf_op jit(solution)/shard_map/pallas_call | solution.py:89
  18.0 1.2 %collective-permute-done.7.rest_1_ = bf16[64,256]{1,0:T(8,128)(2,1)S(1)} collective-permute-done((bf16[64,256]{1,0:T(8,128)(2,1)S(1)}, bf16[64,256]{1,0:T(8,128)(2,1)S(1)}, u32[]{:S(2)}, u32[]{:S(2)}) %collective-permute-start.7) | collective-permute-done | bytes 32800 | tf_op jit(solution)/shard_map/ppermute | solution.py:72
  19.4 0.4 collective-permute-start.10
  19.8 1.7 %collective-permute-start.11 = (bf16[64,256]{1,0:T(8,128)(2,1)S(1)}, bf16[64,256]{1,0:T(8,128)(2,1)S(1)}, u32[]{:S(2)}, u32[]{:S(2)}) collective-permute-start(bf16[64,256]{1,0:T(8,128)(2,1)S(1)} %get-tuple-element.87), channel_id=1, source_target_pairs={{0,1},{1,0},{2,4},{3,5},{4,2},{5,3},{6,7},{7,6},{8,9},{9,8},{10,12... | collective-permute-start | bytes 98312 | tf_op jit(solution)/shard_map/ppermute | solution.py:72
  21.5 1.1 %shard_map.95 = (f32[768,256]{1,0:T(8,128)S(1)}, f32[768,256]{1,0:T(8,128)S(1)}, f32[192,256]{1,0:T(8,128)S(1)}) custom-call(s32[6,3]{1,0:T(8,128)S(1)} %bitcast.30, f32[768,256]{1,0:T(8,128)S(1)} %get-tuple-element.75.state_ref, bf16[768,256]{1,0:T(8,128)(2,1)S(1)} %get-tuple-element.59.inverse_halo_ref, bf16[6,3,128,128]{3,2,1,0:T(8,128)(2,1)S(1)} %bitcast.17, ...), custom_call_target="tpu_custom_call" | custom-call | bytes 2555976 | tf_op jit(solution)/shard_map/pallas_call | solution.py:89
  22.6 0.8 %collective-permute-done.10.rest_1_ = bf16[64,256]{1,0:T(8,128)(2,1)S(1)} collective-permute-done((bf16[64,256]{1,0:T(8,128)(2,1)S(1)}, bf16[64,256]{1,0:T(8,128)(2,1)S(1)}, u32[]{:S(2)}, u32[]{:S(2)}) %collective-permute-start.10) | collective-permute-done | bytes 32800 | tf_op jit(solution)/shard_map/ppermute | solution.py:72
  23.9 1.7 %collective-permute-start.12 = (bf16[64,256]{1,0:T(8,128)(2,1)S(1)}, bf16[64,256]{1,0:T(8,128)(2,1)S(1)}, u32[]{:S(2)}, u32[]{:S(2)}) collective-permute-start(bf16[64,256]{1,0:T(8,128)(2,1)S(1)} %get-tuple-element.90), channel_id=1, source_target_pairs={{0,1},{1,0},{2,3},{3,2},{4,5},{5,4},{6,8},{7,9},{8,6},{9,7},{10,11... | collective-permute-start | bytes 98312 | tf_op jit(solution)/shard_map/ppermute | solution.py:72
  26.0 0.5 shard_map.86
  26.5 1.2 %shard_map.97 = (f32[768,256]{1,0:T(8,128)S(1)}, f32[192,256]{1,0:T(8,128)S(1)}) custom-call(f32[768,256]{1,0:T(8,128)S(1)} %get-tuple-element.82.part_ref, bf16[2,768,256]{2,1,0:T(8,128)(2,1)S(1)} %get-tuple-element.68.blocks_halo_ref, f32[768,256]{1,0:T(8,128)S(1)} %get-tuple-element.83.iterate_ref, bf16[768,1024]{1,0:T(8,128)(2,1)S(1)} %bitcast.13, ...), custom_call_target="tpu_custom_call" | custom-call | bytes 4325376 | tf_op jit(solution)/shard_map/pallas_call | solution.py:89
  27.9 1.7 %collective-permute-done.13.rest_1_ = bf16[64,256]{1,0:T(8,128)(2,1)S(1)} collective-permute-done((bf16[64,256]{1,0:T(8,128)(2,1)S(1)}, bf16[64,256]{1,0:T(8,128)(2,1)S(1)}, u32[]{:S(2)}, u32[]{:S(2)}) %collective-permute-start.13) | collective-permute-done | bytes 32800 | tf_op jit(solution)/shard_map/ppermute | solution.py:72
  30.2 1.7 %collective-permute-start.16 = (bf16[64,256]{1,0:T(8,128)(2,1)S(1)}, bf16[64,256]{1,0:T(8,128)(2,1)S(1)}, u32[]{:S(2)}, u32[]{:S(2)}) collective-permute-start(bf16[64,256]{1,0:T(8,128)(2,1)S(1)} %get-tuple-element.97), channel_id=1, source_target_pairs={{0,1},{1,0},{2,4},{3,5},{4,2},{5,3},{6,7},{7,6},{8,9},{9,8},{10,12... | collective-permute-start | bytes 98312 | tf_op jit(solution)/shard_map/ppermute | solution.py:72
  31.9 1.1 %shard_map.99 = (f32[768,256]{1,0:T(8,128)S(1)}, f32[768,256]{1,0:T(8,128)S(1)}, f32[192,256]{1,0:T(8,128)S(1)}) custom-call(s32[6,3]{1,0:T(8,128)S(1)} %bitcast.31, f32[768,256]{1,0:T(8,128)S(1)} %get-tuple-element.88.state_ref, bf16[768,256]{1,0:T(8,128)(2,1)S(1)} %get-tuple-element.59.inverse_halo_ref, bf16[6,3,128,128]{3,2,1,0:T(8,128)(2,1)S(1)} %bitcast.18, ...), custom_call_target="tpu_custom_call" | custom-call | bytes 2555976 | tf_op jit(solution)/shard_map/pallas_call | solution.py:89
  33.0 0.8 %collective-permute-done.15.rest_0_ = bf16[64,256]{1,0:T(8,128)(2,1)S(1)} collective-permute-done((bf16[64,256]{1,0:T(8,128)(2,1)S(1)}, bf16[64,256]{1,0:T(8,128)(2,1)S(1)}, u32[]{:S(2)}, u32[]{:S(2)}) %collective-permute-start.15) | collective-permute-done | bytes 32800 | tf_op jit(solution)/shard_map/ppermute | solution.py:72
  34.3 1.7 %collective-permute-start.18 = (bf16[64,256]{1,0:T(8,128)(2,1)S(1)}, bf16[64,256]{1,0:T(8,128)(2,1)S(1)}, u32[]{:S(2)}, u32[]{:S(2)}) collective-permute-start(bf16[64,256]{1,0:T(8,128)(2,1)S(1)} %get-tuple-element.102), channel_id=1, source_target_pairs={{0,1},{1,0},{2,3},{3,2},{4,5},{5,4},{6,8},{7,9},{8,6},{9,7},{10,11... | collective-permute-start | bytes 98312 | tf_op jit(solution)/shard_map/ppermute | solution.py:72
  36.4 0.8 %shard_map.101.state_ref = f32[768,256]{1,0:T(8,128)S(1)} custom-call(f32[768,256]{1,0:T(8,128)S(1)} %get-tuple-element.93.part_ref, bf16[2,768,256]{2,1,0:T(8,128)(2,1)S(1)} %get-tuple-element.68.blocks_halo_ref, f32[768,256]{1,0:T(8,128)S(1)} %get-tuple-element.94.iterate_ref, bf16[768,1024]{1,0:T(8,128)(2,1)S(1)} %bitcast.14, ...), custom_call_target="tpu_custom_call" | custom-call | bytes 4325376 | tf_op jit(solution)/shard_map/pallas_call | solution.py:89
  37.2 0.8 %shard_map.102.turned_ref = f32[256,768]{1,0:T(8,128)S(1)} custom-call(f32[768,256]{1,0:T(8,128)S(1)} %shard_map.101.state_ref, bf16[768,768]{1,0:T(8,128)(2,1)S(1)} %get-tuple-element.99.order_ref), custom_call_target="tpu_custom_call" | custom-call | bytes 1966080 | tf_op jit(solution)/shard_map/pallas_call | solution.py:89
  38.3 1.7 %collective-permute-done.19.rest_1_ = bf16[64,256]{1,0:T(8,128)(2,1)S(1)} collective-permute-done((bf16[64,256]{1,0:T(8,128)(2,1)S(1)}, bf16[64,256]{1,0:T(8,128)(2,1)S(1)}, u32[]{:S(2)}, u32[]{:S(2)}) %collective-permute-start.19) | collective-permute-done | bytes 32800 | tf_op jit(solution)/shard_map/ppermute | solution.py:72
  40.3 15.5 %all_to_all.10 = bf16[32,8,768]{2,1,0:T(8,128)(2,1)S(1)} all-to-all(bf16[32,8,768]{2,1,0:T(8,128)(2,1)S(1)} %bitcast.25), channel_id=1, replica_groups=mesh['wide'=16,'narrow'=2] {'narrow','wide'}, dimensions={0} | all-to-all | bytes 786432 | tf_op jit(solution)/shard_map/all_to_all | solution.py:393
  55.8 1.0 %shard_map.105 = (bf16[256,768]{1,0:T(8,128)(2,1)S(1)}, bf16[768,256]{1,0:T(8,128)(2,1)}) custom-call(bf16[256,768]{1,0:T(8,128)(2,1)S(1)} %bitcast.26, bf16[192,192]{1,0:T(8,128)(2,1)S(1)} %get-tuple-element.105.plane_ref, bf16[256,256]{1,0:T(8,128)(2,1)S(1)} %get-tuple-element.106.spread_ref, bf16[256,256]{1,0:T(8,128)(2,1)S(1)} %get-tuple-element.107.vert_ref, ...), custom_call_target="tpu_custom_call" | custom-call | bytes 2007040 | tf_op jit(solution)/shard_map/pallas_call | solution.py:89
  56.9 15.2 %all_to_all.11 = bf16[32,8,768]{2,1,0:T(8,128)(2,1)S(1)} all-to-all(bf16[32,8,768]{2,1,0:T(8,128)(2,1)S(1)} %bitcast.27), channel_id=1, replica_groups=mesh['wide'=16,'narrow'=2] {'narrow','wide'}, dimensions={0} | all-to-all | bytes 786432 | tf_op jit(solution)/shard_map/all_to_all | solution.py:409
  72.1 1.1 %shard_map.106 = bf16[768,256]{1,0:T(8,128)(2,1)} custom-call(bf16[256,768]{1,0:T(8,128)(2,1)S(1)} %bitcast.24), custom_call_target="tpu_custom_call" | custom-call | bytes 393216 | tf_op jit(solution)/shard_map/pallas_call | solution.py:89
  (48 shorter events, 5.6 us)
Async XLA Ops:
  0.6 1.0 %copy-start.2 = (bf16[1,1,768,256]{3,2,1,0:T(8,128)(2,1)S(1)}, bf16[1,1,768,256]{3,2,1,0:T(8,128)(2,1)}, u32[]{:S(2)}) copy-start(bf16[1,1,768,256]{3,2,1,0:T(8,128)(2,1)} %param.7) | copy-start | bytes 1179652
  0.6 0.7 %copy-start.5 = (s32[1,1,4,64]{3,2,1,0:T(4,128)S(1)}, s32[1,1,4,64]{3,2,1,0:T(4,128)}, u32[]{:S(2)}) copy-start(s32[1,1,4,64]{3,2,1,0:T(4,128)} %param.11) | copy-start | bytes 3076
  1.6 4.9 %copy-start.6 = (s32[1,1,6,3]{2,1,3,0:T(1,128)S(1)}, s32[1,1,6,3]{2,1,3,0:T(1,128)}, u32[]{:S(2)}) copy-start(s32[1,1,6,3]{2,1,3,0:T(1,128)} %param.10) | copy-start | bytes 220
  1.6 5.0 %copy-start = (bf16[1,1,768,1024]{3,2,1,0:T(8,128)(2,1)S(1)}, bf16[1,1,768,1024]{3,2,1,0:T(8,128)(2,1)}, u32[]{:S(2)}) copy-start(bf16[1,1,768,1024]{3,2,1,0:T(8,128)(2,1)} %param.8) | copy-start | bytes 4718596
  1.6 5.0 %copy-start.1 = (bf16[1,1,6,3,128,128]{5,4,3,2,1,0:T(8,128)(2,1)S(1)}, bf16[1,1,6,3,128,128]{5,4,3,2,1,0:T(8,128)(2,1)}, u32[]{:S(2)}) copy-start(bf16[1,1,6,3,128,128]{5,4,3,2,1,0:T(8,128)(2,1)} %param.9) | copy-start | bytes 1769476
  1.9 6.3 %collective-permute-start = (bf16[64,256]{1,0:T(8,128)(2,1)S(1)}, bf16[64,256]{1,0:T(8,128)(2,1)S(1)}, u32[]{:S(2)}, u32[]{:S(2)}) collective-permute-start(bf16[64,256]{1,0:T(8,128)(2,1)S(1)} %get-tuple-element.63), channel_id=1, source_target_pairs={{0,1},{1,0},{2,3},{3,2},{4,5},{5,4},{6,8},{7,9},{8,6},{9,7},{10,11... | collective-permute-start | bytes 98312 | tf_op jit(solution)/shard_map/ppermute | solution.py:72
  4.9 3.9 %collective-permute-start.1 = (bf16[64,256]{1,0:T(8,128)(2,1)S(1)}, bf16[64,256]{1,0:T(8,128)(2,1)S(1)}, u32[]{:S(2)}, u32[]{:S(2)}) collective-permute-start(bf16[64,256]{1,0:T(8,128)(2,1)S(1)} %get-tuple-element.64), channel_id=1, source_target_pairs={{0,1},{1,0},{2,4},{3,5},{4,2},{5,3},{6,7},{7,6},{8,9},{9,8},{10,12... | collective-permute-start | bytes 98312 | tf_op jit(solution)/shard_map/ppermute | solution.py:72
  5.0 3.8 %collective-permute-start.2 = (bf16[64,256]{1,0:T(8,128)(2,1)S(1)}, bf16[64,256]{1,0:T(8,128)(2,1)S(1)}, u32[]{:S(2)}, u32[]{:S(2)}) collective-permute-start(bf16[64,256]{1,0:T(8,128)(2,1)S(1)} %get-tuple-element.65), channel_id=1, source_target_pairs={{0,2},{1,3},{2,0},{3,1},{4,6},{5,7},{6,4},{7,5},{8,10},{9,11},{10,... | collective-permute-start | bytes 98312 | tf_op jit(solution)/shard_map/ppermute | solution.py:72
  9.0 4.0 %collective-permute-start.3 = (bf16[64,256]{1,0:T(8,128)(2,1)S(1)}, bf16[64,256]{1,0:T(8,128)(2,1)S(1)}, u32[]{:S(2)}, u32[]{:S(2)}) collective-permute-start(bf16[64,256]{1,0:T(8,128)(2,1)S(1)} %get-tuple-element.72), channel_id=1, source_target_pairs={{0,1},{1,0},{2,3},{3,2},{4,5},{5,4},{6,8},{7,9},{8,6},{9,7},{10,11... | collective-permute-start | bytes 98312 | tf_op jit(solution)/shard_map/ppermute | solution.py:72
  9.4 3.9 %collective-permute-start.4 = (bf16[64,256]{1,0:T(8,128)(2,1)S(1)}, bf16[64,256]{1,0:T(8,128)(2,1)S(1)}, u32[]{:S(2)}, u32[]{:S(2)}) collective-permute-start(bf16[64,256]{1,0:T(8,128)(2,1)S(1)} %get-tuple-element.73), channel_id=1, source_target_pairs={{0,1},{1,0},{2,4},{3,5},{4,2},{5,3},{6,7},{7,6},{8,9},{9,8},{10,12... | collective-permute-start | bytes 98312 | tf_op jit(solution)/shard_map/ppermute | solution.py:72
  11.1 2.2 %collective-permute-start.5 = (bf16[64,256]{1,0:T(8,128)(2,1)S(1)}, bf16[64,256]{1,0:T(8,128)(2,1)S(1)}, u32[]{:S(2)}, u32[]{:S(2)}) collective-permute-start(bf16[64,256]{1,0:T(8,128)(2,1)S(1)} %get-tuple-element.74), channel_id=1, source_target_pairs={{0,2},{1,3},{2,0},{3,1},{4,6},{5,7},{6,4},{7,5},{8,10},{9,11},{10,... | collective-permute-start | bytes 98312 | tf_op jit(solution)/shard_map/ppermute | solution.py:72
  13.5 4.4 %collective-permute-start.6 = (bf16[64,256]{1,0:T(8,128)(2,1)S(1)}, bf16[64,256]{1,0:T(8,128)(2,1)S(1)}, u32[]{:S(2)}, u32[]{:S(2)}) collective-permute-start(bf16[64,256]{1,0:T(8,128)(2,1)S(1)} %get-tuple-element.78), channel_id=1, source_target_pairs={{0,1},{1,0},{2,3},{3,2},{4,5},{5,4},{6,8},{7,9},{8,6},{9,7},{10,11... | collective-permute-start | bytes 98312 | tf_op jit(solution)/shard_map/ppermute | solution.py:72
  15.3 3.9 %collective-permute-start.7 = (bf16[64,256]{1,0:T(8,128)(2,1)S(1)}, bf16[64,256]{1,0:T(8,128)(2,1)S(1)}, u32[]{:S(2)}, u32[]{:S(2)}) collective-permute-start(bf16[64,256]{1,0:T(8,128)(2,1)S(1)} %get-tuple-element.79), channel_id=1, source_target_pairs={{0,1},{1,0},{2,4},{3,5},{4,2},{5,3},{6,7},{7,6},{8,9},{9,8},{10,12... | collective-permute-start | bytes 98312 | tf_op jit(solution)/shard_map/ppermute | solution.py:72
  15.6 3.6 %collective-permute-start.8 = (bf16[64,256]{1,0:T(8,128)(2,1)S(1)}, bf16[64,256]{1,0:T(8,128)(2,1)S(1)}, u32[]{:S(2)}, u32[]{:S(2)}) collective-permute-start(bf16[64,256]{1,0:T(8,128)(2,1)S(1)} %get-tuple-element.80), channel_id=1, source_target_pairs={{0,2},{1,3},{2,0},{3,1},{4,6},{5,7},{6,4},{7,5},{8,10},{9,11},{10,... | collective-permute-start | bytes 98312 | tf_op jit(solution)/shard_map/ppermute | solution.py:72
  19.4 6.7 %copy-start.3 = (bf16[192,192]{1,0:T(8,128)(2,1)S(1)}, bf16[192,192]{1,0:T(8,128)(2,1)}, u32[]{:S(2)}) copy-start(bf16[192,192]{1,0:T(8,128)(2,1)} %cov_plane_ref.1) | copy-start | bytes 221188
  19.4 6.7 %copy-start.4 = (bf16[128,128]{1,0:T(8,128)(2,1)S(1)}, bf16[128,128]{1,0:T(8,128)(2,1)}, u32[]{:S(2)}) copy-start(bf16[128,128]{1,0:T(8,128)(2,1)} %cov_vert_ref.1) | copy-start | bytes 98308
  19.4 4.0 %collective-permute-start.10 = (bf16[64,256]{1,0:T(8,128)(2,1)S(1)}, bf16[64,256]{1,0:T(8,128)(2,1)S(1)}, u32[]{:S(2)}, u32[]{:S(2)}) collective-permute-start(bf16[64,256]{1,0:T(8,128)(2,1)S(1)} %get-tuple-element.86), channel_id=1, source_target_pairs={{0,1},{1,0},{2,3},{3,2},{4,5},{5,4},{6,8},{7,9},{8,6},{9,7},{10,11... | collective-permute-start | bytes 98312 | tf_op jit(solution)/shard_map/ppermute | solution.py:72
  19.8 3.9 %collective-permute-start.11 = (bf16[64,256]{1,0:T(8,128)(2,1)S(1)}, bf16[64,256]{1,0:T(8,128)(2,1)S(1)}, u32[]{:S(2)}, u32[]{:S(2)}) collective-permute-start(bf16[64,256]{1,0:T(8,128)(2,1)S(1)} %get-tuple-element.87), channel_id=1, source_target_pairs={{0,1},{1,0},{2,4},{3,5},{4,2},{5,3},{6,7},{7,6},{8,9},{9,8},{10,12... | collective-permute-start | bytes 98312 | tf_op jit(solution)/shard_map/ppermute | solution.py:72
  21.5 2.2 %collective-permute-start.9 = (bf16[64,256]{1,0:T(8,128)(2,1)S(1)}, bf16[64,256]{1,0:T(8,128)(2,1)S(1)}, u32[]{:S(2)}, u32[]{:S(2)}) collective-permute-start(bf16[64,256]{1,0:T(8,128)(2,1)S(1)} %get-tuple-element.85), channel_id=1, source_target_pairs={{0,2},{1,3},{2,0},{3,1},{4,6},{5,7},{6,4},{7,5},{8,10},{9,11},{10,... | collective-permute-start | bytes 98312 | tf_op jit(solution)/shard_map/ppermute | solution.py:72
  23.9 4.0 %collective-permute-start.12 = (bf16[64,256]{1,0:T(8,128)(2,1)S(1)}, bf16[64,256]{1,0:T(8,128)(2,1)S(1)}, u32[]{:S(2)}, u32[]{:S(2)}) collective-permute-start(bf16[64,256]{1,0:T(8,128)(2,1)S(1)} %get-tuple-element.90), channel_id=1, source_target_pairs={{0,1},{1,0},{2,3},{3,2},{4,5},{5,4},{6,8},{7,9},{8,6},{9,7},{10,11... | collective-permute-start | bytes 98312 | tf_op jit(solution)/shard_map/ppermute | solution.py:72
  25.7 3.9 %collective-permute-start.13 = (bf16[64,256]{1,0:T(8,128)(2,1)S(1)}, bf16[64,256]{1,0:T(8,128)(2,1)S(1)}, u32[]{:S(2)}, u32[]{:S(2)}) collective-permute-start(bf16[64,256]{1,0:T(8,128)(2,1)S(1)} %get-tuple-element.91), channel_id=1, source_target_pairs={{0,1},{1,0},{2,4},{3,5},{4,2},{5,3},{6,7},{7,6},{8,9},{9,8},{10,12... | collective-permute-start | bytes 98312 | tf_op jit(solution)/shard_map/ppermute | solution.py:72
  26.0 3.6 %collective-permute-start.14 = (bf16[64,256]{1,0:T(8,128)(2,1)S(1)}, bf16[64,256]{1,0:T(8,128)(2,1)S(1)}, u32[]{:S(2)}, u32[]{:S(2)}) collective-permute-start(bf16[64,256]{1,0:T(8,128)(2,1)S(1)} %get-tuple-element.92), channel_id=1, source_target_pairs={{0,2},{1,3},{2,0},{3,1},{4,6},{5,7},{6,4},{7,5},{8,10},{9,11},{10,... | collective-permute-start | bytes 98312 | tf_op jit(solution)/shard_map/ppermute | solution.py:72
  29.8 4.0 %collective-permute-start.15 = (bf16[64,256]{1,0:T(8,128)(2,1)S(1)}, bf16[64,256]{1,0:T(8,128)(2,1)S(1)}, u32[]{:S(2)}, u32[]{:S(2)}) collective-permute-start(bf16[64,256]{1,0:T(8,128)(2,1)S(1)} %get-tuple-element.96), channel_id=1, source_target_pairs={{0,1},{1,0},{2,3},{3,2},{4,5},{5,4},{6,8},{7,9},{8,6},{9,7},{10,11... | collective-permute-start | bytes 98312 | tf_op jit(solution)/shard_map/ppermute | solution.py:72
  30.2 3.9 %collective-permute-start.16 = (bf16[64,256]{1,0:T(8,128)(2,1)S(1)}, bf16[64,256]{1,0:T(8,128)(2,1)S(1)}, u32[]{:S(2)}, u32[]{:S(2)}) collective-permute-start(bf16[64,256]{1,0:T(8,128)(2,1)S(1)} %get-tuple-element.97), channel_id=1, source_target_pairs={{0,1},{1,0},{2,4},{3,5},{4,2},{5,3},{6,7},{7,6},{8,9},{9,8},{10,12... | collective-permute-start | bytes 98312 | tf_op jit(solution)/shard_map/ppermute | solution.py:72
  31.9 2.2 %collective-permute-start.17 = (bf16[64,256]{1,0:T(8,128)(2,1)S(1)}, bf16[64,256]{1,0:T(8,128)(2,1)S(1)}, u32[]{:S(2)}, u32[]{:S(2)}) collective-permute-start(bf16[64,256]{1,0:T(8,128)(2,1)S(1)} %get-tuple-element.98), channel_id=1, source_target_pairs={{0,2},{1,3},{2,0},{3,1},{4,6},{5,7},{6,4},{7,5},{8,10},{9,11},{10,... | collective-permute-start | bytes 98312 | tf_op jit(solution)/shard_map/ppermute | solution.py:72
  34.3 4.0 %collective-permute-start.18 = (bf16[64,256]{1,0:T(8,128)(2,1)S(1)}, bf16[64,256]{1,0:T(8,128)(2,1)S(1)}, u32[]{:S(2)}, u32[]{:S(2)}) collective-permute-start(bf16[64,256]{1,0:T(8,128)(2,1)S(1)} %get-tuple-element.102), channel_id=1, source_target_pairs={{0,1},{1,0},{2,3},{3,2},{4,5},{5,4},{6,8},{7,9},{8,6},{9,7},{10,11... | collective-permute-start | bytes 98312 | tf_op jit(solution)/shard_map/ppermute | solution.py:72
  36.1 3.9 %collective-permute-start.19 = (bf16[64,256]{1,0:T(8,128)(2,1)S(1)}, bf16[64,256]{1,0:T(8,128)(2,1)S(1)}, u32[]{:S(2)}, u32[]{:S(2)}) collective-permute-start(bf16[64,256]{1,0:T(8,128)(2,1)S(1)} %get-tuple-element.103), channel_id=1, source_target_pairs={{0,1},{1,0},{2,4},{3,5},{4,2},{5,3},{6,7},{7,6},{8,9},{9,8},{10,12... | collective-permute-start | bytes 98312 | tf_op jit(solution)/shard_map/ppermute | solution.py:72
  36.4 3.6 %collective-permute-start.20 = (bf16[64,256]{1,0:T(8,128)(2,1)S(1)}, bf16[64,256]{1,0:T(8,128)(2,1)S(1)}, u32[]{:S(2)}, u32[]{:S(2)}) collective-permute-start(bf16[64,256]{1,0:T(8,128)(2,1)S(1)} %get-tuple-element.104), channel_id=1, source_target_pairs={{0,2},{1,3},{2,0},{3,1},{4,6},{5,7},{6,4},{7,5},{8,10},{9,11},{10,... | collective-permute-start | bytes 98312 | tf_op jit(solution)/shard_map/ppermute | solution.py:72

commit v3 on v2

--- a/solution.py
+++ b/solution.py
@@ -246,7 +246,11 @@
 
 def wire_body(count, turned_ref, halo_table_ref, *rest):
     got, (wire_ref,) = rest[:count], rest[count:]
-    wire_ref[...] = (turned_ref[...] + mm(join_halo(got).T, halo_table_ref[...])).astype(BF)
+    halo = jnp.concatenate([piece[...] for piece in got], axis=0)
+    part = lax.dot_general(
+        halo, halo_table_ref[:halo.shape[0], :], (((0,), (0,)), ((), ())), preferred_element_type=F32
+    )
+    wire_ref[...] = (turned_ref[...] + part).astype(BF)
 
 
 def one_hot(rows_of, shape):

time: 73.4 us -> 73.4 us (level)
  no operation moved by 1% of the time
where the time goes in v3:
time: 73.4 us; the launch traced here: 73.2 us
  blocking collectives  30.8 us (42%)
  starting transfers between devices  17.7 us (24%)
  Pallas kernels  13.8 us (19%)
  waiting for transfers between devices  9.09 us (12%)
  local copies, waits for them, and re-layouts  0.97 us (1%)
  between operations  0.83 us (1%)
    ppermute x21, starting transfers between devices, swap(): lax.ppermute(m, ('wide', 'narrow'), list(f[-1]))  17.7 us
    all_to_all x1, blocking collectives, smooth_by_columns(): lax.all_to_all(wire.reshape(devices, group, own), ('narrow', 'wide'), spl...  15.5 us
    all_to_all x1, blocking collectives, smooth_by_columns(): lax.all_to_all(mixed.reshape(devices, group, own), ('narrow', 'wide'), sp...  15.2 us
    pallas_call x21, Pallas kernels, call(): pl.pallas_call(body, out_shape=outs, in_specs=specs or [VM] * len(args),...  13.8 us
    ppermute x21, waiting for transfers between devices, swap(): lax.ppermute(m, ('wide', 'narrow'), list(f[-1]))  9.09 us
  transfers between devices with their start and end apart: 21, of which 12 were waited for; matrix products, arithmetic and copies ran while one was open for 0% of the time, Pallas kernels for 14%

profile of v3, /device:TPU:0, one launch (start us, length us, event | category | flops | bytes accessed | tf_op | source)
XLA Modules:
  0.0 73.2 jit_solution(10571874608097875005)
XLA Ops:
  0.6 0.7 copy-done.5
  1.9 3.0 %collective-permute-start = (bf16[64,256]{1,0:T(8,128)(2,1)S(1)}, bf16[64,256]{1,0:T(8,128)(2,1)S(1)}, u32[]{:S(2)}, u32[]{:S(2)}) collective-permute-start(bf16[64,256]{1,0:T(8,128)(2,1)S(1)} %get-tuple-element.63), channel_id=1, source_target_pairs={{0,1},{1,0},{2,3},{3,2},{4,5},{5,4},{6,8},{7,9},{8,6},{9,7},{10,11... | collective-permute-start | bytes 98312 | tf_op jit(solution)/shard_map/ppermute | solution.py:72
  5.0 1.6 %collective-permute-start.2 = (bf16[64,256]{1,0:T(8,128)(2,1)S(1)}, bf16[64,256]{1,0:T(8,128)(2,1)S(1)}, u32[]{:S(2)}, u32[]{:S(2)}) collective-permute-start(bf16[64,256]{1,0:T(8,128)(2,1)S(1)} %get-tuple-element.65), channel_id=1, source_target_pairs={{0,2},{1,3},{2,0},{3,1},{4,6},{5,7},{6,4},{7,5},{8,10},{9,11},{10,... | collective-permute-start | bytes 98312 | tf_op jit(solution)/shard_map/ppermute | solution.py:72
  6.6 1.6 %shard_map.88 = (bf16[768,256]{1,0:T(8,128)(2,1)S(1)}, bf16[2,768,256]{2,1,0:T(8,128)(2,1)S(1)}, bf16[192,256]{1,0:T(8,128)(2,1)S(1)}, bf16[384,256]{1,0:T(8,128...) custom-call(s32[6,3]{1,0:T(8,128)S(1)} %bitcast.28, bf16[768,1024]{1,0:T(8,128)(2,1)S(1)} %bitcast.11, ...), custom_call_target="tpu_custom_call" | custom-call | bytes 2850888 | tf_op jit(solution)/shard_map/pallas_call | solution.py:89
  8.2 0.6 collective-permute-done.1.rest_1_
  9.4 1.7 %collective-permute-start.4 = (bf16[64,256]{1,0:T(8,128)(2,1)S(1)}, bf16[64,256]{1,0:T(8,128)(2,1)S(1)}, u32[]{:S(2)}, u32[]{:S(2)}) collective-permute-start(bf16[64,256]{1,0:T(8,128)(2,1)S(1)} %get-tuple-element.73), channel_id=1, source_target_pairs={{0,1},{1,0},{2,4},{3,5},{4,2},{5,3},{6,7},{7,6},{8,9},{9,8},{10,12... | collective-permute-start | bytes 98312 | tf_op jit(solution)/shard_map/ppermute | solution.py:72
  11.1 1.1 %shard_map.91 = (f32[768,256]{1,0:T(8,128)S(1)}, f32[768,256]{1,0:T(8,128)S(1)}, f32[192,256]{1,0:T(8,128)S(1)}) custom-call(s32[6,3]{1,0:T(8,128)S(1)} %bitcast.29, f32[768,256]{1,0:T(8,128)S(1)} %get-tuple-element.62.state_ref, bf16[768,256]{1,0:T(8,128)(2,1)S(1)} %get-tuple-element.59.inverse_halo_ref, bf16[6,3,128,128]{3,2,1,0:T(8,128)(2,1)S(1)} %bitcast.16, ...), custom_call_target="tpu_custom_call" | custom-call | bytes 2555976 | tf_op jit(solution)/shard_map/pallas_call | solution.py:89
  12.2 0.8 %collective-permute-done.3.rest_0_ = bf16[64,256]{1,0:T(8,128)(2,1)S(1)} collective-permute-done((bf16[64,256]{1,0:T(8,128)(2,1)S(1)}, bf16[64,256]{1,0:T(8,128)(2,1)S(1)}, u32[]{:S(2)}, u32[]{:S(2)}) %collective-permute-start.3) | collective-permute-done | bytes 32800 | tf_op jit(solution)/shard_map/ppermute | solution.py:72
  13.5 1.7 %collective-permute-start.6 = (bf16[64,256]{1,0:T(8,128)(2,1)S(1)}, bf16[64,256]{1,0:T(8,128)(2,1)S(1)}, u32[]{:S(2)}, u32[]{:S(2)}) collective-permute-start(bf16[64,256]{1,0:T(8,128)(2,1)S(1)} %get-tuple-element.78), channel_id=1, source_target_pairs={{0,1},{1,0},{2,3},{3,2},{4,5},{5,4},{6,8},{7,9},{8,6},{9,7},{10,11... | collective-permute-start | bytes 98312 | tf_op jit(solution)/shard_map/ppermute | solution.py:72
  15.6 0.5 collective-permute-start.8
  16.1 0.7 shard_map.89
  16.8 1.2 %shard_map.93 = (f32[768,256]{1,0:T(8,128)S(1)}, f32[192,256]{1,0:T(8,128)S(1)}) custom-call(f32[768,256]{1,0:T(8,128)S(1)} %get-tuple-element.67.part_ref, bf16[2,768,256]{2,1,0:T(8,128)(2,1)S(1)} %get-tuple-element.68.blocks_halo_ref, f32[768,256]{1,0:T(8,128)S(1)} %get-tuple-element.69.iterate_ref, bf16[768,1024]{1,0:T(8,128)(2,1)S(1)} %bitcast.12, ...), custom_call_target="tpu_custom_call" | custom-call | bytes 4325376 | tf_op jit(solution)/shard_map/pallas_call | solution.py:89
  18.0 1.2 %collective-permute-done.7.rest_1_ = bf16[64,256]{1,0:T(8,128)(2,1)S(1)} collective-permute-done((bf16[64,256]{1,0:T(8,128)(2,1)S(1)}, bf16[64,256]{1,0:T(8,128)(2,1)S(1)}, u32[]{:S(2)}, u32[]{:S(2)}) %collective-permute-start.7) | collective-permute-done | bytes 32800 | tf_op jit(solution)/shard_map/ppermute | solution.py:72
  19.4 0.4 collective-permute-start.10
  19.8 1.7 %collective-permute-start.11 = (bf16[64,256]{1,0:T(8,128)(2,1)S(1)}, bf16[64,256]{1,0:T(8,128)(2,1)S(1)}, u32[]{:S(2)}, u32[]{:S(2)}) collective-permute-start(bf16[64,256]{1,0:T(8,128)(2,1)S(1)} %get-tuple-element.87), channel_id=1, source_target_pairs={{0,1},{1,0},{2,4},{3,5},{4,2},{5,3},{6,7},{7,6},{8,9},{9,8},{10,12... | collective-permute-start | bytes 98312 | tf_op jit(solution)/shard_map/ppermute | solution.py:72
  21.5 1.1 %shard_map.95 = (f32[768,256]{1,0:T(8,128)S(1)}, f32[768,256]{1,0:T(8,128)S(1)}, f32[192,256]{1,0:T(8,128)S(1)}) custom-call(s32[6,3]{1,0:T(8,128)S(1)} %bitcast.30, f32[768,256]{1,0:T(8,128)S(1)} %get-tuple-element.75.state_ref, bf16[768,256]{1,0:T(8,128)(2,1)S(1)} %get-tuple-element.59.inverse_halo_ref, bf16[6,3,128,128]{3,2,1,0:T(8,128)(2,1)S(1)} %bitcast.17, ...), custom_call_target="tpu_custom_call" | custom-call | bytes 2555976 | tf_op jit(solution)/shard_map/pallas_call | solution.py:89
  22.6 0.8 %collective-permute-done.10.rest_1_ = bf16[64,256]{1,0:T(8,128)(2,1)S(1)} collective-permute-done((bf16[64,256]{1,0:T(8,128)(2,1)S(1)}, bf16[64,256]{1,0:T(8,128)(2,1)S(1)}, u32[]{:S(2)}, u32[]{:S(2)}) %collective-permute-start.10) | collective-permute-done | bytes 32800 | tf_op jit(solution)/shard_map/ppermute | solution.py:72
  23.9 1.7 %collective-permute-start.12 = (bf16[64,256]{1,0:T(8,128)(2,1)S(1)}, bf16[64,256]{1,0:T(8,128)(2,1)S(1)}, u32[]{:S(2)}, u32[]{:S(2)}) collective-permute-start(bf16[64,256]{1,0:T(8,128)(2,1)S(1)} %get-tuple-element.90), channel_id=1, source_target_pairs={{0,1},{1,0},{2,3},{3,2},{4,5},{5,4},{6,8},{7,9},{8,6},{9,7},{10,11... | collective-permute-start | bytes 98312 | tf_op jit(solution)/shard_map/ppermute | solution.py:72
  26.0 0.5 shard_map.86
  26.5 1.2 %shard_map.97 = (f32[768,256]{1,0:T(8,128)S(1)}, f32[192,256]{1,0:T(8,128)S(1)}) custom-call(f32[768,256]{1,0:T(8,128)S(1)} %get-tuple-element.82.part_ref, bf16[2,768,256]{2,1,0:T(8,128)(2,1)S(1)} %get-tuple-element.68.blocks_halo_ref, f32[768,256]{1,0:T(8,128)S(1)} %get-tuple-element.83.iterate_ref, bf16[768,1024]{1,0:T(8,128)(2,1)S(1)} %bitcast.13, ...), custom_call_target="tpu_custom_call" | custom-call | bytes 4325376 | tf_op jit(solution)/shard_map/pallas_call | solution.py:89
  27.9 1.7 %collective-permute-done.13.rest_1_ = bf16[64,256]{1,0:T(8,128)(2,1)S(1)} collective-permute-done((bf16[64,256]{1,0:T(8,128)(2,1)S(1)}, bf16[64,256]{1,0:T(8,128)(2,1)S(1)}, u32[]{:S(2)}, u32[]{:S(2)}) %collective-permute-start.13) | collective-permute-done | bytes 32800 | tf_op jit(solution)/shard_map/ppermute | solution.py:72
  30.2 1.7 %collective-permute-start.16 = (bf16[64,256]{1,0:T(8,128)(2,1)S(1)}, bf16[64,256]{1,0:T(8,128)(2,1)S(1)}, u32[]{:S(2)}, u32[]{:S(2)}) collective-permute-start(bf16[64,256]{1,0:T(8,128)(2,1)S(1)} %get-tuple-element.97), channel_id=1, source_target_pairs={{0,1},{1,0},{2,4},{3,5},{4,2},{5,3},{6,7},{7,6},{8,9},{9,8},{10,12... | collective-permute-start | bytes 98312 | tf_op jit(solution)/shard_map/ppermute | solution.py:72
  31.9 1.1 %shard_map.99 = (f32[768,256]{1,0:T(8,128)S(1)}, f32[768,256]{1,0:T(8,128)S(1)}, f32[192,256]{1,0:T(8,128)S(1)}) custom-call(s32[6,3]{1,0:T(8,128)S(1)} %bitcast.31, f32[768,256]{1,0:T(8,128)S(1)} %get-tuple-element.88.state_ref, bf16[768,256]{1,0:T(8,128)(2,1)S(1)} %get-tuple-element.59.inverse_halo_ref, bf16[6,3,128,128]{3,2,1,0:T(8,128)(2,1)S(1)} %bitcast.18, ...), custom_call_target="tpu_custom_call" | custom-call | bytes 2555976 | tf_op jit(solution)/shard_map/pallas_call | solution.py:89
  33.0 0.8 %collective-permute-done.15.rest_0_ = bf16[64,256]{1,0:T(8,128)(2,1)S(1)} collective-permute-done((bf16[64,256]{1,0:T(8,128)(2,1)S(1)}, bf16[64,256]{1,0:T(8,128)(2,1)S(1)}, u32[]{:S(2)}, u32[]{:S(2)}) %collective-permute-start.15) | collective-permute-done | bytes 32800 | tf_op jit(solution)/shard_map/ppermute | solution.py:72
  34.3 1.7 %collective-permute-start.18 = (bf16[64,256]{1,0:T(8,128)(2,1)S(1)}, bf16[64,256]{1,0:T(8,128)(2,1)S(1)}, u32[]{:S(2)}, u32[]{:S(2)}) collective-permute-start(bf16[64,256]{1,0:T(8,128)(2,1)S(1)} %get-tuple-element.102), channel_id=1, source_target_pairs={{0,1},{1,0},{2,3},{3,2},{4,5},{5,4},{6,8},{7,9},{8,6},{9,7},{10,11... | collective-permute-start | bytes 98312 | tf_op jit(solution)/shard_map/ppermute | solution.py:72
  36.4 0.8 %shard_map.101.state_ref = f32[768,256]{1,0:T(8,128)S(1)} custom-call(f32[768,256]{1,0:T(8,128)S(1)} %get-tuple-element.93.part_ref, bf16[2,768,256]{2,1,0:T(8,128)(2,1)S(1)} %get-tuple-element.68.blocks_halo_ref, f32[768,256]{1,0:T(8,128)S(1)} %get-tuple-element.94.iterate_ref, bf16[768,1024]{1,0:T(8,128)(2,1)S(1)} %bitcast.14, ...), custom_call_target="tpu_custom_call" | custom-call | bytes 4325376 | tf_op jit(solution)/shard_map/pallas_call | solution.py:89
  37.2 0.8 %shard_map.102.turned_ref = f32[256,768]{1,0:T(8,128)S(1)} custom-call(f32[768,256]{1,0:T(8,128)S(1)} %shard_map.101.state_ref, bf16[768,768]{1,0:T(8,128)(2,1)S(1)} %get-tuple-element.99.order_ref), custom_call_target="tpu_custom_call" | custom-call | bytes 1966080 | tf_op jit(solution)/shard_map/pallas_call | solution.py:89
  38.3 1.7 %collective-permute-done.19.rest_1_ = bf16[64,256]{1,0:T(8,128)(2,1)S(1)} collective-permute-done((bf16[64,256]{1,0:T(8,128)(2,1)S(1)}, bf16[64,256]{1,0:T(8,128)(2,1)S(1)}, u32[]{:S(2)}, u32[]{:S(2)}) %collective-permute-start.19) | collective-permute-done | bytes 32800 | tf_op jit(solution)/shard_map/ppermute | solution.py:72
  40.3 15.5 %all_to_all.10 = bf16[32,8,768]{2,1,0:T(8,128)(2,1)S(1)} all-to-all(bf16[32,8,768]{2,1,0:T(8,128)(2,1)S(1)} %bitcast.25), channel_id=1, replica_groups=mesh['wide'=16,'narrow'=2] {'narrow','wide'}, dimensions={0} | all-to-all | bytes 786432 | tf_op jit(solution)/shard_map/all_to_all | solution.py:397
  55.8 1.0 %shard_map.105 = (bf16[256,768]{1,0:T(8,128)(2,1)S(1)}, bf16[768,256]{1,0:T(8,128)(2,1)}) custom-call(bf16[256,768]{1,0:T(8,128)(2,1)S(1)} %bitcast.26, bf16[192,192]{1,0:T(8,128)(2,1)S(1)} %get-tuple-element.105.plane_ref, bf16[256,256]{1,0:T(8,128)(2,1)S(1)} %get-tuple-element.106.spread_ref, bf16[256,256]{1,0:T(8,128)(2,1)S(1)} %get-tuple-element.107.vert_ref, ...), custom_call_target="tpu_custom_call" | custom-call | bytes 2007040 | tf_op jit(solution)/shard_map/pallas_call | solution.py:89
  56.9 15.2 %all_to_all.11 = bf16[32,8,768]{2,1,0:T(8,128)(2,1)S(1)} all-to-all(bf16[32,8,768]{2,1,0:T(8,128)(2,1)S(1)} %bitcast.27), channel_id=1, replica_groups=mesh['wide'=16,'narrow'=2] {'narrow','wide'}, dimensions={0} | all-to-all | bytes 786432 | tf_op jit(solution)/shard_map/all_to_all | solution.py:413
  72.1 1.1 %shard_map.106 = bf16[768,256]{1,0:T(8,128)(2,1)} custom-call(bf16[256,768]{1,0:T(8,128)(2,1)S(1)} %bitcast.24), custom_call_target="tpu_custom_call" | custom-call | bytes 393216 | tf_op jit(solution)/shard_map/pallas_call | solution.py:89
  (48 shorter events, 5.6 us)
Async XLA Ops:
  0.6 1.0 %copy-start.2 = (bf16[1,1,768,256]{3,2,1,0:T(8,128)(2,1)S(1)}, bf16[1,1,768,256]{3,2,1,0:T(8,128)(2,1)}, u32[]{:S(2)}) copy-start(bf16[1,1,768,256]{3,2,1,0:T(8,128)(2,1)} %param.7) | copy-start | bytes 1179652
  0.6 0.7 %copy-start.5 = (s32[1,1,4,64]{3,2,1,0:T(4,128)S(1)}, s32[1,1,4,64]{3,2,1,0:T(4,128)}, u32[]{:S(2)}) copy-start(s32[1,1,4,64]{3,2,1,0:T(4,128)} %param.11) | copy-start | bytes 3076
  1.6 4.9 %copy-start.6 = (s32[1,1,6,3]{2,1,3,0:T(1,128)S(1)}, s32[1,1,6,3]{2,1,3,0:T(1,128)}, u32[]{:S(2)}) copy-start(s32[1,1,6,3]{2,1,3,0:T(1,128)} %param.10) | copy-start | bytes 220
  1.6 5.0 %copy-start = (bf16[1,1,768,1024]{3,2,1,0:T(8,128)(2,1)S(1)}, bf16[1,1,768,1024]{3,2,1,0:T(8,128)(2,1)}, u32[]{:S(2)}) copy-start(bf16[1,1,768,1024]{3,2,1,0:T(8,128)(2,1)} %param.8) | copy-start | bytes 4718596
  1.6 5.0 %copy-start.1 = (bf16[1,1,6,3,128,128]{5,4,3,2,1,0:T(8,128)(2,1)S(1)}, bf16[1,1,6,3,128,128]{5,4,3,2,1,0:T(8,128)(2,1)}, u32[]{:S(2)}) copy-start(bf16[1,1,6,3,128,128]{5,4,3,2,1,0:T(8,128)(2,1)} %param.9) | copy-start | bytes 1769476
  1.9 6.3 %collective-permute-start = (bf16[64,256]{1,0:T(8,128)(2,1)S(1)}, bf16[64,256]{1,0:T(8,128)(2,1)S(1)}, u32[]{:S(2)}, u32[]{:S(2)}) collective-permute-start(bf16[64,256]{1,0:T(8,128)(2,1)S(1)} %get-tuple-element.63), channel_id=1, source_target_pairs={{0,1},{1,0},{2,3},{3,2},{4,5},{5,4},{6,8},{7,9},{8,6},{9,7},{10,11... | collective-permute-start | bytes 98312 | tf_op jit(solution)/shard_map/ppermute | solution.py:72
  4.9 3.9 %collective-permute-start.1 = (bf16[64,256]{1,0:T(8,128)(2,1)S(1)}, bf16[64,256]{1,0:T(8,128)(2,1)S(1)}, u32[]{:S(2)}, u32[]{:S(2)}) collective-permute-start(bf16[64,256]{1,0:T(8,128)(2,1)S(1)} %get-tuple-element.64), channel_id=1, source_target_pairs={{0,1},{1,0},{2,4},{3,5},{4,2},{5,3},{6,7},{7,6},{8,9},{9,8},{10,12... | collective-permute-start | bytes 98312 | tf_op jit(solution)/shard_map/ppermute | solution.py:72
  5.0 3.8 %collective-permute-start.2 = (bf16[64,256]{1,0:T(8,128)(2,1)S(1)}, bf16[64,256]{1,0:T(8,128)(2,1)S(1)}, u32[]{:S(2)}, u32[]{:S(2)}) collective-permute-start(bf16[64,256]{1,0:T(8,128)(2,1)S(1)} %get-tuple-element.65), channel_id=1, source_target_pairs={{0,2},{1,3},{2,0},{3,1},{4,6},{5,7},{6,4},{7,5},{8,10},{9,11},{10,... | collective-permute-start | bytes 98312 | tf_op jit(solution)/shard_map/ppermute | solution.py:72
  9.0 4.0 %collective-permute-start.3 = (bf16[64,256]{1,0:T(8,128)(2,1)S(1)}, bf16[64,256]{1,0:T(8,128)(2,1)S(1)}, u32[]{:S(2)}, u32[]{:S(2)}) collective-permute-start(bf16[64,256]{1,0:T(8,128)(2,1)S(1)} %get-tuple-element.72), channel_id=1, source_target_pairs={{0,1},{1,0},{2,3},{3,2},{4,5},{5,4},{6,8},{7,9},{8,6},{9,7},{10,11... | collective-permute-start | bytes 98312 | tf_op jit(solution)/shard_map/ppermute | solution.py:72
  9.4 3.9 %collective-permute-start.4 = (bf16[64,256]{1,0:T(8,128)(2,1)S(1)}, bf16[64,256]{1,0:T(8,128)(2,1)S(1)}, u32[]{:S(2)}, u32[]{:S(2)}) collective-permute-start(bf16[64,256]{1,0:T(8,128)(2,1)S(1)} %get-tuple-element.73), channel_id=1, source_target_pairs={{0,1},{1,0},{2,4},{3,5},{4,2},{5,3},{6,7},{7,6},{8,9},{9,8},{10,12... | collective-permute-start | bytes 98312 | tf_op jit(solution)/shard_map/ppermute | solution.py:72
  11.1 2.2 %collective-permute-start.5 = (bf16[64,256]{1,0:T(8,128)(2,1)S(1)}, bf16[64,256]{1,0:T(8,128)(2,1)S(1)}, u32[]{:S(2)}, u32[]{:S(2)}) collective-permute-start(bf16[64,256]{1,0:T(8,128)(2,1)S(1)} %get-tuple-element.74), channel_id=1, source_target_pairs={{0,2},{1,3},{2,0},{3,1},{4,6},{5,7},{6,4},{7,5},{8,10},{9,11},{10,... | collective-permute-start | bytes 98312 | tf_op jit(solution)/shard_map/ppermute | solution.py:72
  13.5 4.4 %collective-permute-start.6 = (bf16[64,256]{1,0:T(8,128)(2,1)S(1)}, bf16[64,256]{1,0:T(8,128)(2,1)S(1)}, u32[]{:S(2)}, u32[]{:S(2)}) collective-permute-start(bf16[64,256]{1,0:T(8,128)(2,1)S(1)} %get-tuple-element.78), channel_id=1, source_target_pairs={{0,1},{1,0},{2,3},{3,2},{4,5},{5,4},{6,8},{7,9},{8,6},{9,7},{10,11... | collective-permute-start | bytes 98312 | tf_op jit(solution)/shard_map/ppermute | solution.py:72
  15.3 3.9 %collective-permute-start.7 = (bf16[64,256]{1,0:T(8,128)(2,1)S(1)}, bf16[64,256]{1,0:T(8,128)(2,1)S(1)}, u32[]{:S(2)}, u32[]{:S(2)}) collective-permute-start(bf16[64,256]{1,0:T(8,128)(2,1)S(1)} %get-tuple-element.79), channel_id=1, source_target_pairs={{0,1},{1,0},{2,4},{3,5},{4,2},{5,3},{6,7},{7,6},{8,9},{9,8},{10,12... | collective-permute-start | bytes 98312 | tf_op jit(solution)/shard_map/ppermute | solution.py:72
  15.6 3.6 %collective-permute-start.8 = (bf16[64,256]{1,0:T(8,128)(2,1)S(1)}, bf16[64,256]{1,0:T(8,128)(2,1)S(1)}, u32[]{:S(2)}, u32[]{:S(2)}) collective-permute-start(bf16[64,256]{1,0:T(8,128)(2,1)S(1)} %get-tuple-element.80), channel_id=1, source_target_pairs={{0,2},{1,3},{2,0},{3,1},{4,6},{5,7},{6,4},{7,5},{8,10},{9,11},{10,... | collective-permute-start | bytes 98312 | tf_op jit(solution)/shard_map/ppermute | solution.py:72
  19.4 6.7 %copy-start.3 = (bf16[192,192]{1,0:T(8,128)(2,1)S(1)}, bf16[192,192]{1,0:T(8,128)(2,1)}, u32[]{:S(2)}) copy-start(bf16[192,192]{1,0:T(8,128)(2,1)} %cov_plane_ref.1) | copy-start | bytes 221188
  19.4 6.7 %copy-start.4 = (bf16[128,128]{1,0:T(8,128)(2,1)S(1)}, bf16[128,128]{1,0:T(8,128)(2,1)}, u32[]{:S(2)}) copy-start(bf16[128,128]{1,0:T(8,128)(2,1)} %cov_vert_ref.1) | copy-start | bytes 98308
  19.4 4.0 %collective-permute-start.10 = (bf16[64,256]{1,0:T(8,128)(2,1)S(1)}, bf16[64,256]{1,0:T(8,128)(2,1)S(1)}, u32[]{:S(2)}, u32[]{:S(2)}) collective-permute-start(bf16[64,256]{1,0:T(8,128)(2,1)S(1)} %get-tuple-element.86), channel_id=1, source_target_pairs={{0,1},{1,0},{2,3},{3,2},{4,5},{5,4},{6,8},{7,9},{8,6},{9,7},{10,11... | collective-permute-start | bytes 98312 | tf_op jit(solution)/shard_map/ppermute | solution.py:72
  19.8 3.9 %collective-permute-start.11 = (bf16[64,256]{1,0:T(8,128)(2,1)S(1)}, bf16[64,256]{1,0:T(8,128)(2,1)S(1)}, u32[]{:S(2)}, u32[]{:S(2)}) collective-permute-start(bf16[64,256]{1,0:T(8,128)(2,1)S(1)} %get-tuple-element.87), channel_id=1, source_target_pairs={{0,1},{1,0},{2,4},{3,5},{4,2},{5,3},{6,7},{7,6},{8,9},{9,8},{10,12... | collective-permute-start | bytes 98312 | tf_op jit(solution)/shard_map/ppermute | solution.py:72
  21.5 2.2 %collective-permute-start.9 = (bf16[64,256]{1,0:T(8,128)(2,1)S(1)}, bf16[64,256]{1,0:T(8,128)(2,1)S(1)}, u32[]{:S(2)}, u32[]{:S(2)}) collective-permute-start(bf16[64,256]{1,0:T(8,128)(2,1)S(1)} %get-tuple-element.85), channel_id=1, source_target_pairs={{0,2},{1,3},{2,0},{3,1},{4,6},{5,7},{6,4},{7,5},{8,10},{9,11},{10,... | collective-permute-start | bytes 98312 | tf_op jit(solution)/shard_map/ppermute | solution.py:72
  23.9 4.0 %collective-permute-start.12 = (bf16[64,256]{1,0:T(8,128)(2,1)S(1)}, bf16[64,256]{1,0:T(8,128)(2,1)S(1)}, u32[]{:S(2)}, u32[]{:S(2)}) collective-permute-start(bf16[64,256]{1,0:T(8,128)(2,1)S(1)} %get-tuple-element.90), channel_id=1, source_target_pairs={{0,1},{1,0},{2,3},{3,2},{4,5},{5,4},{6,8},{7,9},{8,6},{9,7},{10,11... | collective-permute-start | bytes 98312 | tf_op jit(solution)/shard_map/ppermute | solution.py:72
  25.7 3.9 %collective-permute-start.13 = (bf16[64,256]{1,0:T(8,128)(2,1)S(1)}, bf16[64,256]{1,0:T(8,128)(2,1)S(1)}, u32[]{:S(2)}, u32[]{:S(2)}) collective-permute-start(bf16[64,256]{1,0:T(8,128)(2,1)S(1)} %get-tuple-element.91), channel_id=1, source_target_pairs={{0,1},{1,0},{2,4},{3,5},{4,2},{5,3},{6,7},{7,6},{8,9},{9,8},{10,12... | collective-permute-start | bytes 98312 | tf_op jit(solution)/shard_map/ppermute | solution.py:72
  26.0 3.6 %collective-permute-start.14 = (bf16[64,256]{1,0:T(8,128)(2,1)S(1)}, bf16[64,256]{1,0:T(8,128)(2,1)S(1)}, u32[]{:S(2)}, u32[]{:S(2)}) collective-permute-start(bf16[64,256]{1,0:T(8,128)(2,1)S(1)} %get-tuple-element.92), channel_id=1, source_target_pairs={{0,2},{1,3},{2,0},{3,1},{4,6},{5,7},{6,4},{7,5},{8,10},{9,11},{10,... | collective-permute-start | bytes 98312 | tf_op jit(solution)/shard_map/ppermute | solution.py:72
  29.8 4.0 %collective-permute-start.15 = (bf16[64,256]{1,0:T(8,128)(2,1)S(1)}, bf16[64,256]{1,0:T(8,128)(2,1)S(1)}, u32[]{:S(2)}, u32[]{:S(2)}) collective-permute-start(bf16[64,256]{1,0:T(8,128)(2,1)S(1)} %get-tuple-element.96), channel_id=1, source_target_pairs={{0,1},{1,0},{2,3},{3,2},{4,5},{5,4},{6,8},{7,9},{8,6},{9,7},{10,11... | collective-permute-start | bytes 98312 | tf_op jit(solution)/shard_map/ppermute | solution.py:72
  30.2 3.9 %collective-permute-start.16 = (bf16[64,256]{1,0:T(8,128)(2,1)S(1)}, bf16[64,256]{1,0:T(8,128)(2,1)S(1)}, u32[]{:S(2)}, u32[]{:S(2)}) collective-permute-start(bf16[64,256]{1,0:T(8,128)(2,1)S(1)} %get-tuple-element.97), channel_id=1, source_target_pairs={{0,1},{1,0},{2,4},{3,5},{4,2},{5,3},{6,7},{7,6},{8,9},{9,8},{10,12... | collective-permute-start | bytes 98312 | tf_op jit(solution)/shard_map/ppermute | solution.py:72
  31.9 2.2 %collective-permute-start.17 = (bf16[64,256]{1,0:T(8,128)(2,1)S(1)}, bf16[64,256]{1,0:T(8,128)(2,1)S(1)}, u32[]{:S(2)}, u32[]{:S(2)}) collective-permute-start(bf16[64,256]{1,0:T(8,128)(2,1)S(1)} %get-tuple-element.98), channel_id=1, source_target_pairs={{0,2},{1,3},{2,0},{3,1},{4,6},{5,7},{6,4},{7,5},{8,10},{9,11},{10,... | collective-permute-start | bytes 98312 | tf_op jit(solution)/shard_map/ppermute | solution.py:72
  34.3 4.0 %collective-permute-start.18 = (bf16[64,256]{1,0:T(8,128)(2,1)S(1)}, bf16[64,256]{1,0:T(8,128)(2,1)S(1)}, u32[]{:S(2)}, u32[]{:S(2)}) collective-permute-start(bf16[64,256]{1,0:T(8,128)(2,1)S(1)} %get-tuple-element.102), channel_id=1, source_target_pairs={{0,1},{1,0},{2,3},{3,2},{4,5},{5,4},{6,8},{7,9},{8,6},{9,7},{10,11... | collective-permute-start | bytes 98312 | tf_op jit(solution)/shard_map/ppermute | solution.py:72
  36.1 3.9 %collective-permute-start.19 = (bf16[64,256]{1,0:T(8,128)(2,1)S(1)}, bf16[64,256]{1,0:T(8,128)(2,1)S(1)}, u32[]{:S(2)}, u32[]{:S(2)}) collective-permute-start(bf16[64,256]{1,0:T(8,128)(2,1)S(1)} %get-tuple-element.103), channel_id=1, source_target_pairs={{0,1},{1,0},{2,4},{3,5},{4,2},{5,3},{6,7},{7,6},{8,9},{9,8},{10,12... | collective-permute-start | bytes 98312 | tf_op jit(solution)/shard_map/ppermute | solution.py:72
  36.4 3.6 %collective-permute-start.20 = (bf16[64,256]{1,0:T(8,128)(2,1)S(1)}, bf16[64,256]{1,0:T(8,128)(2,1)S(1)}, u32[]{:S(2)}, u32[]{:S(2)}) collective-permute-start(bf16[64,256]{1,0:T(8,128)(2,1)S(1)} %get-tuple-element.104), channel_id=1, source_target_pairs={{0,2},{1,3},{2,0},{3,1},{4,6},{5,7},{6,4},{7,5},{8,10},{9,11},{10,... | collective-permute-start | bytes 98312 | tf_op jit(solution)/shard_map/ppermute | solution.py:72
